TPU v7x, 512 devices: a whole 4x4x16 slice. The times are simulated.
512 devices in a mesh: tm: 32 (over y, x, core), space: 16 (over z).
Axes of the slice: x: 4, y: 4, z: 16, core: 2. Of those that a mesh axis runs over, the one named last changes fastest.
Arguments:
- initial: float32 [256, 8, 512], P('space'), may hold values from -6 to 6
- stale_start: float32 [256, 8, 512], P('space'), may hold values from -6 to 6
- guess: float32 [32, 256, 8, 512], P('tm', 'space'), may hold values from -6 to 6
- forcing: float32 [256, 8, 512], P('space'), may hold values from -8 to 8
- wall_class: int32 [256, 8, 512], P('space'), may hold values from 0 to 3
- damping_table: float32 [4], replicated, may hold values from 0.01 to 0.25
- coarse_prop: float32 [512, 512], replicated, may hold values from -1 to 1
Outputs:
- corrected: float32 [32, 256, 8, 512], P('tm', 'space')
- residual_norm: float32 [32], P('tm')
All inputs are finite; a program needn't handle non-finite values.
Results may differ from a plain program's by a relative error of at most 0.00015.
Values sent between devices are 32-bit elements; how exact they have to be, the bound alone decides.
A program may use at most 128 MiB of HBM per device.

v0:
```python
import jax
import jax.numpy as jnp
from jax import lax
from jax.sharding import PartitionSpec as P

STEPS = 4
CLASSES = 4


coupling = 0.12


def padded(cells, sides, width):
    for axis, dim in sides:
        count = lax.axis_size(axis)
        head = lax.slice_in_dim(cells, 0, width, axis=dim)
        tail = lax.slice_in_dim(cells, cells.shape[dim] - width, cells.shape[dim], axis=dim)
        cells = jnp.concatenate(
            [
                lax.ppermute(tail, axis, [(i, (i + 1) % count) for i in range(count)]),
                cells,
                lax.ppermute(head, axis, [((i + 1) % count, i) for i in range(count)]),
            ],
            axis=dim,
        )
    return cells


def shifted(block, axis, distance):
    devices = range(lax.axis_size(axis))
    route = [(i - distance, i) for i in devices if i - distance in devices]
    return lax.ppermute(block, axis, route)


def advance(wide, damping, forcing):
    field = wide[1:-1]
    stream = wide[2:] + wide[:-2] - 2.0 * field
    padded_y = jnp.pad(field, ((0, 0), (1, 1), (0, 0)))
    beside_y = padded_y[:, 2:] + padded_y[:, :-2] - 2.0 * field
    padded_z = jnp.pad(field, ((0, 0), (0, 0), (1, 1)))
    beside_z = padded_z[:, :, 2:] + padded_z[:, :, :-2] - 2.0 * field
    return field + coupling * (stream + beside_y + beside_z) - damping * field + forcing


def sweep(field, damping, forcing):
    for sweep_step in range(STEPS):
        wide = padded(field, (("space", 0),), 1)
        field = advance(wide, damping, forcing)
    return field


def shards(initial, stale_start, guess, forcing, wall_class, damping_table, coarse_prop):
    damping = jnp.zeros(wall_class.shape, jnp.float32)
    for class_no in range(CLASSES):
        damping = damping + jnp.where(
            wall_class == class_no, damping_table[class_no], jnp.float32(0.0)
        )
    first_slice = lax.axis_index("tm") == 0
    earlier_guess = shifted(guess[0], "tm", 1)
    start = jnp.where(first_slice, stale_start, earlier_guess)
    relaxed = sweep(start, damping, forcing)
    earlier_value = shifted(relaxed, "tm", 1)
    again = jnp.where(first_slice, initial, earlier_value)
    residual = sweep(again, damping, forcing) - relaxed
    width = coarse_prop.shape[0]
    flat = residual.reshape(-1, width)

    def turn(turn_no, error):
        before = shifted(error, "tm", 1)
        return jnp.dot(before, coarse_prop, precision=lax.Precision.HIGHEST) + flat

    error = lax.fori_loop(0, lax.axis_size("tm") - 1, turn, flat)
    corrected = relaxed + error.reshape(relaxed.shape)
    squares = lax.psum(jnp.sum(residual * residual), "space")
    count = residual.size * lax.axis_size("space")
    norm = jnp.sqrt(squares / count).reshape(1)
    return (corrected[None], norm)


def solution(mesh):
    return jax.shard_map(
        shards,
        mesh=mesh,
        in_specs=(
            P("space", None, None),
            P("space", None, None),
            P("tm", "space", None, None),
            P("space", None, None),
            P("space", None, None),
            P(),
            P(),
        ),
        out_specs=(P("tm", "space", None, None), P("tm")),
        check_vma=False,
    )
```

profile of v0, /device:TPU:24, one launch (start us, length us, event | category | flops | bytes accessed | tf_op | source)
XLA Modules:
  0.0 483.4 jit_solution(15990987446265564789)
XLA Ops:
  2.6 8.1 %collective-permute-done.1 = f32[16,8,512]{2,1,0:T(8,128)S(1)} collective-permute-done((f32[16,8,512]{2,1,0:T(8,128)}, f32[16,8,512]{2,1,0:T(8,128)S(1)}, u32[]{:S(2)}, u32[]{:S(2)}) %collective-permute-start.1) | collective-permute-done | bytes 262176 | tf_op jit(solution)/shard_map/ppermute | solution.py:32
  10.7 11.4 %collective-permute-start.2 = (f32[1,8,512]{2,1,0:T(8,128)S(1)}, f32[1,8,512]{2,1,0:T(8,128)S(1)}, u32[]{:S(2)}, u32[]{:S(2)}) collective-permute-start(f32[1,8,512]{2,1,0:T(8,128)S(1)} %get-tuple-element.49), channel_id=1, source_target_pairs={{1,0},{2,1},{3,2},{4,3},{5,4},{6,5},{7,6},{8,7},{9,8},{10,9},{11,1... | collective-permute-start | bytes 49160 | tf_op jit(solution)/shard_map/ppermute | solution.py:22
  69.7 7.9 %collective-permute-done.10 = f32[16,8,512]{2,1,0:T(8,128)S(1)} collective-permute-done((f32[16,8,512]{2,1,0:T(8,128)S(1)}, f32[16,8,512]{2,1,0:T(8,128)S(1)}, u32[]{:S(2)}, u32[]{:S(2)}) %collective-permute-start.10) | collective-permute-done | bytes 262176 | tf_op jit(solution)/shard_map/ppermute | solution.py:32
  125.8 28.4 %psum.7 = f32[]{:T(128)} all-reduce(f32[]{:T(128)} %get-tuple-element.33), channel_id=1, replica_groups=mesh['tm'=32,'space'=16] {'space'}, use_global_device_ids=true, to_apply=%region_3.4 | all-reduce | flops 1 | bytes 8 | tf_op jit(solution)/shard_map/psum | solution.py:74
  154.9 326.6 %while.10 = (s32[]{:T(128)}, f32[128,512]{1,0:T(8,128)S(1)}, f32[512,512]{1,0:T(8,128)S(1)}, f32[128,512]{1,0:T(8,128)S(1)}, s32[]{:T(128)}) while((s32[]{:T(128)}, f32[128,512]{1,0:T(8,128)S(1)}, f32[512,512]{1,0:T(8,128)S(1)}, f32[128,512]{1,0:T(8,128)S(1)}, s32[]{:T(128)}) %tuple.38), condition=%wide.region_1.2_spmd, body=%wide.region_0.1_spmd.sunk | while | flops 402718720 | bytes 2883685 | solution.py:72
  156.9 7.9 %collective-permute-done = f32[128,512]{1,0:T(8,128)S(1)} collective-permute-done((f32[128,512]{1,0:T(8,128)S(1)}, f32[128,512]{1,0:T(8,128)S(1)}, u32[]{:S(2)}, u32[]{:S(2)}) %collective-permute-start) | collective-permute-done | bytes 262176 | tf_op jit(solution)/shard_map/while/body/eval_jaxpr/ppermute | solution.py:32
  167.4 7.9 %collective-permute-done = f32[128,512]{1,0:T(8,128)S(1)} collective-permute-done((f32[128,512]{1,0:T(8,128)S(1)}, f32[128,512]{1,0:T(8,128)S(1)}, u32[]{:S(2)}, u32[]{:S(2)}) %collective-permute-start) | collective-permute-done | bytes 262176 | tf_op jit(solution)/shard_map/while/body/eval_jaxpr/ppermute | solution.py:32
  177.9 7.9 %collective-permute-done = f32[128,512]{1,0:T(8,128)S(1)} collective-permute-done((f32[128,512]{1,0:T(8,128)S(1)}, f32[128,512]{1,0:T(8,128)S(1)}, u32[]{:S(2)}, u32[]{:S(2)}) %collective-permute-start) | collective-permute-done | bytes 262176 | tf_op jit(solution)/shard_map/while/body/eval_jaxpr/ppermute | solution.py:32
  188.5 7.9 %collective-permute-done = f32[128,512]{1,0:T(8,128)S(1)} collective-permute-done((f32[128,512]{1,0:T(8,128)S(1)}, f32[128,512]{1,0:T(8,128)S(1)}, u32[]{:S(2)}, u32[]{:S(2)}) %collective-permute-start) | collective-permute-done | bytes 262176 | tf_op jit(solution)/shard_map/while/body/eval_jaxpr/ppermute | solution.py:32
  199.0 7.9 %collective-permute-done = f32[128,512]{1,0:T(8,128)S(1)} collective-permute-done((f32[128,512]{1,0:T(8,128)S(1)}, f32[128,512]{1,0:T(8,128)S(1)}, u32[]{:S(2)}, u32[]{:S(2)}) %collective-permute-start) | collective-permute-done | bytes 262176 | tf_op jit(solution)/shard_map/while/body/eval_jaxpr/ppermute | solution.py:32
  209.6 7.9 %collective-permute-done = f32[128,512]{1,0:T(8,128)S(1)} collective-permute-done((f32[128,512]{1,0:T(8,128)S(1)}, f32[128,512]{1,0:T(8,128)S(1)}, u32[]{:S(2)}, u32[]{:S(2)}) %collective-permute-start) | collective-permute-done | bytes 262176 | tf_op jit(solution)/shard_map/while/body/eval_jaxpr/ppermute | solution.py:32
  220.1 7.9 %collective-permute-done = f32[128,512]{1,0:T(8,128)S(1)} collective-permute-done((f32[128,512]{1,0:T(8,128)S(1)}, f32[128,512]{1,0:T(8,128)S(1)}, u32[]{:S(2)}, u32[]{:S(2)}) %collective-permute-start) | collective-permute-done | bytes 262176 | tf_op jit(solution)/shard_map/while/body/eval_jaxpr/ppermute | solution.py:32
  230.6 7.9 %collective-permute-done = f32[128,512]{1,0:T(8,128)S(1)} collective-permute-done((f32[128,512]{1,0:T(8,128)S(1)}, f32[128,512]{1,0:T(8,128)S(1)}, u32[]{:S(2)}, u32[]{:S(2)}) %collective-permute-start) | collective-permute-done | bytes 262176 | tf_op jit(solution)/shard_map/while/body/eval_jaxpr/ppermute | solution.py:32
  241.2 7.9 %collective-permute-done = f32[128,512]{1,0:T(8,128)S(1)} collective-permute-done((f32[128,512]{1,0:T(8,128)S(1)}, f32[128,512]{1,0:T(8,128)S(1)}, u32[]{:S(2)}, u32[]{:S(2)}) %collective-permute-start) | collective-permute-done | bytes 262176 | tf_op jit(solution)/shard_map/while/body/eval_jaxpr/ppermute | solution.py:32
  251.7 7.9 %collective-permute-done = f32[128,512]{1,0:T(8,128)S(1)} collective-permute-done((f32[128,512]{1,0:T(8,128)S(1)}, f32[128,512]{1,0:T(8,128)S(1)}, u32[]{:S(2)}, u32[]{:S(2)}) %collective-permute-start) | collective-permute-done | bytes 262176 | tf_op jit(solution)/shard_map/while/body/eval_jaxpr/ppermute | solution.py:32
  262.2 7.9 %collective-permute-done = f32[128,512]{1,0:T(8,128)S(1)} collective-permute-done((f32[128,512]{1,0:T(8,128)S(1)}, f32[128,512]{1,0:T(8,128)S(1)}, u32[]{:S(2)}, u32[]{:S(2)}) %collective-permute-start) | collective-permute-done | bytes 262176 | tf_op jit(solution)/shard_map/while/body/eval_jaxpr/ppermute | solution.py:32
  272.8 7.9 %collective-permute-done = f32[128,512]{1,0:T(8,128)S(1)} collective-permute-done((f32[128,512]{1,0:T(8,128)S(1)}, f32[128,512]{1,0:T(8,128)S(1)}, u32[]{:S(2)}, u32[]{:S(2)}) %collective-permute-start) | collective-permute-done | bytes 262176 | tf_op jit(solution)/shard_map/while/body/eval_jaxpr/ppermute | solution.py:32
  283.3 7.9 %collective-permute-done = f32[128,512]{1,0:T(8,128)S(1)} collective-permute-done((f32[128,512]{1,0:T(8,128)S(1)}, f32[128,512]{1,0:T(8,128)S(1)}, u32[]{:S(2)}, u32[]{:S(2)}) %collective-permute-start) | collective-permute-done | bytes 262176 | tf_op jit(solution)/shard_map/while/body/eval_jaxpr/ppermute | solution.py:32
  293.8 7.9 %collective-permute-done = f32[128,512]{1,0:T(8,128)S(1)} collective-permute-done((f32[128,512]{1,0:T(8,128)S(1)}, f32[128,512]{1,0:T(8,128)S(1)}, u32[]{:S(2)}, u32[]{:S(2)}) %collective-permute-start) | collective-permute-done | bytes 262176 | tf_op jit(solution)/shard_map/while/body/eval_jaxpr/ppermute | solution.py:32
  304.4 7.9 %collective-permute-done = f32[128,512]{1,0:T(8,128)S(1)} collective-permute-done((f32[128,512]{1,0:T(8,128)S(1)}, f32[128,512]{1,0:T(8,128)S(1)}, u32[]{:S(2)}, u32[]{:S(2)}) %collective-permute-start) | collective-permute-done | bytes 262176 | tf_op jit(solution)/shard_map/while/body/eval_jaxpr/ppermute | solution.py:32
  325.4 7.9 %collective-permute-done = f32[128,512]{1,0:T(8,128)S(1)} collective-permute-done((f32[128,512]{1,0:T(8,128)S(1)}, f32[128,512]{1,0:T(8,128)S(1)}, u32[]{:S(2)}, u32[]{:S(2)}) %collective-permute-start) | collective-permute-done | bytes 262176 | tf_op jit(solution)/shard_map/while/body/eval_jaxpr/ppermute | solution.py:32
  336.0 7.9 %collective-permute-done = f32[128,512]{1,0:T(8,128)S(1)} collective-permute-done((f32[128,512]{1,0:T(8,128)S(1)}, f32[128,512]{1,0:T(8,128)S(1)}, u32[]{:S(2)}, u32[]{:S(2)}) %collective-permute-start) | collective-permute-done | bytes 262176 | tf_op jit(solution)/shard_map/while/body/eval_jaxpr/ppermute | solution.py:32
  388.6 7.9 %collective-permute-done = f32[128,512]{1,0:T(8,128)S(1)} collective-permute-done((f32[128,512]{1,0:T(8,128)S(1)}, f32[128,512]{1,0:T(8,128)S(1)}, u32[]{:S(2)}, u32[]{:S(2)}) %collective-permute-start) | collective-permute-done | bytes 262176 | tf_op jit(solution)/shard_map/while/body/eval_jaxpr/ppermute | solution.py:32
  451.9 7.9 %collective-permute-done = f32[128,512]{1,0:T(8,128)S(1)} collective-permute-done((f32[128,512]{1,0:T(8,128)S(1)}, f32[128,512]{1,0:T(8,128)S(1)}, u32[]{:S(2)}, u32[]{:S(2)}) %collective-permute-start) | collective-permute-done | bytes 262176 | tf_op jit(solution)/shard_map/while/body/eval_jaxpr/ppermute | solution.py:32
  (138 shorter events, 274.3 us)
Async XLA Ops:
  0.6 10.0 %collective-permute-start.1 = (f32[16,8,512]{2,1,0:T(8,128)}, f32[16,8,512]{2,1,0:T(8,128)S(1)}, u32[]{:S(2)}, u32[]{:S(2)}) collective-permute-start(f32[16,8,512]{2,1,0:T(8,128)} %bitcast.21), channel_id=1, source_target_pairs={{0,16},{16,32},{32,48},{48,64},{64,80},{80,96},{96,112},{112,128},... | collective-permute-start | bytes 786440 | tf_op jit(solution)/shard_map/ppermute | solution.py:32
  10.7 14.0 %collective-permute-start.2 = (f32[1,8,512]{2,1,0:T(8,128)S(1)}, f32[1,8,512]{2,1,0:T(8,128)S(1)}, u32[]{:S(2)}, u32[]{:S(2)}) collective-permute-start(f32[1,8,512]{2,1,0:T(8,128)S(1)} %get-tuple-element.49), channel_id=1, source_target_pairs={{1,0},{2,1},{3,2},{4,3},{5,4},{6,5},{7,6},{8,7},{9,8},{10,9},{11,1... | collective-permute-start | bytes 49160 | tf_op jit(solution)/shard_map/ppermute | solution.py:22
  67.7 9.8 %collective-permute-start.10 = (f32[16,8,512]{2,1,0:T(8,128)S(1)}, f32[16,8,512]{2,1,0:T(8,128)S(1)}, u32[]{:S(2)}, u32[]{:S(2)}) collective-permute-start(f32[16,8,512]{2,1,0:T(8,128)S(1)} %fusion.27), channel_id=1, source_target_pairs={{0,16},{16,32},{32,48},{48,64},{64,80},{80,96},{96,112},{112,128},... | collective-permute-start | bytes 786440 | tf_op jit(solution)/shard_map/ppermute | solution.py:32
  155.0 9.8 %collective-permute-start = (f32[128,512]{1,0:T(8,128)S(1)}, f32[128,512]{1,0:T(8,128)S(1)}, u32[]{:S(2)}, u32[]{:S(2)}) collective-permute-start(f32[128,512]{1,0:T(8,128)S(1)} %get-tuple-element.86), channel_id=1, source_target_pairs={{0,16},{16,32},{32,48},{48,64},{64,80},{80,96},{96,112},{112,128},... | collective-permute-start | bytes 786440 | tf_op jit(solution)/shard_map/while/body/eval_jaxpr/ppermute | solution.py:32
  165.5 9.8 %collective-permute-start = (f32[128,512]{1,0:T(8,128)S(1)}, f32[128,512]{1,0:T(8,128)S(1)}, u32[]{:S(2)}, u32[]{:S(2)}) collective-permute-start(f32[128,512]{1,0:T(8,128)S(1)} %get-tuple-element.86), channel_id=1, source_target_pairs={{0,16},{16,32},{32,48},{48,64},{64,80},{80,96},{96,112},{112,128},... | collective-permute-start | bytes 786440 | tf_op jit(solution)/shard_map/while/body/eval_jaxpr/ppermute | solution.py:32
  176.0 9.8 %collective-permute-start = (f32[128,512]{1,0:T(8,128)S(1)}, f32[128,512]{1,0:T(8,128)S(1)}, u32[]{:S(2)}, u32[]{:S(2)}) collective-permute-start(f32[128,512]{1,0:T(8,128)S(1)} %get-tuple-element.86), channel_id=1, source_target_pairs={{0,16},{16,32},{32,48},{48,64},{64,80},{80,96},{96,112},{112,128},... | collective-permute-start | bytes 786440 | tf_op jit(solution)/shard_map/while/body/eval_jaxpr/ppermute | solution.py:32
  186.6 9.8 %collective-permute-start = (f32[128,512]{1,0:T(8,128)S(1)}, f32[128,512]{1,0:T(8,128)S(1)}, u32[]{:S(2)}, u32[]{:S(2)}) collective-permute-start(f32[128,512]{1,0:T(8,128)S(1)} %get-tuple-element.86), channel_id=1, source_target_pairs={{0,16},{16,32},{32,48},{48,64},{64,80},{80,96},{96,112},{112,128},... | collective-permute-start | bytes 786440 | tf_op jit(solution)/shard_map/while/body/eval_jaxpr/ppermute | solution.py:32
  197.1 9.8 %collective-permute-start = (f32[128,512]{1,0:T(8,128)S(1)}, f32[128,512]{1,0:T(8,128)S(1)}, u32[]{:S(2)}, u32[]{:S(2)}) collective-permute-start(f32[128,512]{1,0:T(8,128)S(1)} %get-tuple-element.86), channel_id=1, source_target_pairs={{0,16},{16,32},{32,48},{48,64},{64,80},{80,96},{96,112},{112,128},... | collective-permute-start | bytes 786440 | tf_op jit(solution)/shard_map/while/body/eval_jaxpr/ppermute | solution.py:32
  207.6 9.8 %collective-permute-start = (f32[128,512]{1,0:T(8,128)S(1)}, f32[128,512]{1,0:T(8,128)S(1)}, u32[]{:S(2)}, u32[]{:S(2)}) collective-permute-start(f32[128,512]{1,0:T(8,128)S(1)} %get-tuple-element.86), channel_id=1, source_target_pairs={{0,16},{16,32},{32,48},{48,64},{64,80},{80,96},{96,112},{112,128},... | collective-permute-start | bytes 786440 | tf_op jit(solution)/shard_map/while/body/eval_jaxpr/ppermute | solution.py:32
  218.2 9.8 %collective-permute-start = (f32[128,512]{1,0:T(8,128)S(1)}, f32[128,512]{1,0:T(8,128)S(1)}, u32[]{:S(2)}, u32[]{:S(2)}) collective-permute-start(f32[128,512]{1,0:T(8,128)S(1)} %get-tuple-element.86), channel_id=1, source_target_pairs={{0,16},{16,32},{32,48},{48,64},{64,80},{80,96},{96,112},{112,128},... | collective-permute-start | bytes 786440 | tf_op jit(solution)/shard_map/while/body/eval_jaxpr/ppermute | solution.py:32
  228.7 9.8 %collective-permute-start = (f32[128,512]{1,0:T(8,128)S(1)}, f32[128,512]{1,0:T(8,128)S(1)}, u32[]{:S(2)}, u32[]{:S(2)}) collective-permute-start(f32[128,512]{1,0:T(8,128)S(1)} %get-tuple-element.86), channel_id=1, source_target_pairs={{0,16},{16,32},{32,48},{48,64},{64,80},{80,96},{96,112},{112,128},... | collective-permute-start | bytes 786440 | tf_op jit(solution)/shard_map/while/body/eval_jaxpr/ppermute | solution.py:32
  239.2 9.8 %collective-permute-start = (f32[128,512]{1,0:T(8,128)S(1)}, f32[128,512]{1,0:T(8,128)S(1)}, u32[]{:S(2)}, u32[]{:S(2)}) collective-permute-start(f32[128,512]{1,0:T(8,128)S(1)} %get-tuple-element.86), channel_id=1, source_target_pairs={{0,16},{16,32},{32,48},{48,64},{64,80},{80,96},{96,112},{112,128},... | collective-permute-start | bytes 786440 | tf_op jit(solution)/shard_map/while/body/eval_jaxpr/ppermute | solution.py:32
  249.8 9.8 %collective-permute-start = (f32[128,512]{1,0:T(8,128)S(1)}, f32[128,512]{1,0:T(8,128)S(1)}, u32[]{:S(2)}, u32[]{:S(2)}) collective-permute-start(f32[128,512]{1,0:T(8,128)S(1)} %get-tuple-element.86), channel_id=1, source_target_pairs={{0,16},{16,32},{32,48},{48,64},{64,80},{80,96},{96,112},{112,128},... | collective-permute-start | bytes 786440 | tf_op jit(solution)/shard_map/while/body/eval_jaxpr/ppermute | solution.py:32
  260.3 9.8 %collective-permute-start = (f32[128,512]{1,0:T(8,128)S(1)}, f32[128,512]{1,0:T(8,128)S(1)}, u32[]{:S(2)}, u32[]{:S(2)}) collective-permute-start(f32[128,512]{1,0:T(8,128)S(1)} %get-tuple-element.86), channel_id=1, source_target_pairs={{0,16},{16,32},{32,48},{48,64},{64,80},{80,96},{96,112},{112,128},... | collective-permute-start | bytes 786440 | tf_op jit(solution)/shard_map/while/body/eval_jaxpr/ppermute | solution.py:32
  270.8 9.8 %collective-permute-start = (f32[128,512]{1,0:T(8,128)S(1)}, f32[128,512]{1,0:T(8,128)S(1)}, u32[]{:S(2)}, u32[]{:S(2)}) collective-permute-start(f32[128,512]{1,0:T(8,128)S(1)} %get-tuple-element.86), channel_id=1, source_target_pairs={{0,16},{16,32},{32,48},{48,64},{64,80},{80,96},{96,112},{112,128},... | collective-permute-start | bytes 786440 | tf_op jit(solution)/shard_map/while/body/eval_jaxpr/ppermute | solution.py:32
  281.4 9.8 %collective-permute-start = (f32[128,512]{1,0:T(8,128)S(1)}, f32[128,512]{1,0:T(8,128)S(1)}, u32[]{:S(2)}, u32[]{:S(2)}) collective-permute-start(f32[128,512]{1,0:T(8,128)S(1)} %get-tuple-element.86), channel_id=1, source_target_pairs={{0,16},{16,32},{32,48},{48,64},{64,80},{80,96},{96,112},{112,128},... | collective-permute-start | bytes 786440 | tf_op jit(solution)/shard_map/while/body/eval_jaxpr/ppermute | solution.py:32
  291.9 9.8 %collective-permute-start = (f32[128,512]{1,0:T(8,128)S(1)}, f32[128,512]{1,0:T(8,128)S(1)}, u32[]{:S(2)}, u32[]{:S(2)}) collective-permute-start(f32[128,512]{1,0:T(8,128)S(1)} %get-tuple-element.86), channel_id=1, source_target_pairs={{0,16},{16,32},{32,48},{48,64},{64,80},{80,96},{96,112},{112,128},... | collective-permute-start | bytes 786440 | tf_op jit(solution)/shard_map/while/body/eval_jaxpr/ppermute | solution.py:32
  302.4 9.8 %collective-permute-start = (f32[128,512]{1,0:T(8,128)S(1)}, f32[128,512]{1,0:T(8,128)S(1)}, u32[]{:S(2)}, u32[]{:S(2)}) collective-permute-start(f32[128,512]{1,0:T(8,128)S(1)} %get-tuple-element.86), channel_id=1, source_target_pairs={{0,16},{16,32},{32,48},{48,64},{64,80},{80,96},{96,112},{112,128},... | collective-permute-start | bytes 786440 | tf_op jit(solution)/shard_map/while/body/eval_jaxpr/ppermute | solution.py:32
  313.0 9.8 %collective-permute-start = (f32[128,512]{1,0:T(8,128)S(1)}, f32[128,512]{1,0:T(8,128)S(1)}, u32[]{:S(2)}, u32[]{:S(2)}) collective-permute-start(f32[128,512]{1,0:T(8,128)S(1)} %get-tuple-element.86), channel_id=1, source_target_pairs={{0,16},{16,32},{32,48},{48,64},{64,80},{80,96},{96,112},{112,128},... | collective-permute-start | bytes 786440 | tf_op jit(solution)/shard_map/while/body/eval_jaxpr/ppermute | solution.py:32
  323.5 9.8 %collective-permute-start = (f32[128,512]{1,0:T(8,128)S(1)}, f32[128,512]{1,0:T(8,128)S(1)}, u32[]{:S(2)}, u32[]{:S(2)}) collective-permute-start(f32[128,512]{1,0:T(8,128)S(1)} %get-tuple-element.86), channel_id=1, source_target_pairs={{0,16},{16,32},{32,48},{48,64},{64,80},{80,96},{96,112},{112,128},... | collective-permute-start | bytes 786440 | tf_op jit(solution)/shard_map/while/body/eval_jaxpr/ppermute | solution.py:32
  334.0 9.8 %collective-permute-start = (f32[128,512]{1,0:T(8,128)S(1)}, f32[128,512]{1,0:T(8,128)S(1)}, u32[]{:S(2)}, u32[]{:S(2)}) collective-permute-start(f32[128,512]{1,0:T(8,128)S(1)} %get-tuple-element.86), channel_id=1, source_target_pairs={{0,16},{16,32},{32,48},{48,64},{64,80},{80,96},{96,112},{112,128},... | collective-permute-start | bytes 786440 | tf_op jit(solution)/shard_map/while/body/eval_jaxpr/ppermute | solution.py:32
  386.7 9.8 %collective-permute-start = (f32[128,512]{1,0:T(8,128)S(1)}, f32[128,512]{1,0:T(8,128)S(1)}, u32[]{:S(2)}, u32[]{:S(2)}) collective-permute-start(f32[128,512]{1,0:T(8,128)S(1)} %get-tuple-element.86), channel_id=1, source_target_pairs={{0,16},{16,32},{32,48},{48,64},{64,80},{80,96},{96,112},{112,128},... | collective-permute-start | bytes 786440 | tf_op jit(solution)/shard_map/while/body/eval_jaxpr/ppermute | solution.py:32
  397.3 9.8 %collective-permute-start = (f32[128,512]{1,0:T(8,128)S(1)}, f32[128,512]{1,0:T(8,128)S(1)}, u32[]{:S(2)}, u32[]{:S(2)}) collective-permute-start(f32[128,512]{1,0:T(8,128)S(1)} %get-tuple-element.86), channel_id=1, source_target_pairs={{0,16},{16,32},{32,48},{48,64},{64,80},{80,96},{96,112},{112,128},... | collective-permute-start | bytes 786440 | tf_op jit(solution)/shard_map/while/body/eval_jaxpr/ppermute | solution.py:32
  449.9 9.8 %collective-permute-start = (f32[128,512]{1,0:T(8,128)S(1)}, f32[128,512]{1,0:T(8,128)S(1)}, u32[]{:S(2)}, u32[]{:S(2)}) collective-permute-start(f32[128,512]{1,0:T(8,128)S(1)} %get-tuple-element.86), channel_id=1, source_target_pairs={{0,16},{16,32},{32,48},{48,64},{64,80},{80,96},{96,112},{112,128},... | collective-permute-start | bytes 786440 | tf_op jit(solution)/shard_map/while/body/eval_jaxpr/ppermute | solution.py:32
  (30 other events, 321.6 us)
where the time goes:
time: 485 us; the launch traced here: 483 us
  waiting for transfers between devices  286 us (59%)
  starting transfers between devices  118 us (24%)
  blocking collectives  28.4 us (6%)
  other arithmetic  24.4 us (5%)
  matrix products  22 us (5%)
    ppermute x33, waiting for transfers between devices, shifted(): return lax.ppermute(block, axis, route)  260 us
    ppermute x33, starting transfers between devices, shifted(): return lax.ppermute(block, axis, route)  63.4 us
    psum x1, blocking collectives, shards(): squares = lax.psum(jnp.sum(residual * residual), 'space')  28.4 us
    ppermute x8, starting transfers between devices, padded(): lax.ppermute(tail, axis, [(i, (i + 1) % count) for i in range(count)])  27.9 us
    ppermute x8, starting transfers between devices, padded(): lax.ppermute(head, axis, [((i + 1) % count, i) for i in range(count)])  26.5 us
    ppermute x8, waiting for transfers between devices, padded(): lax.ppermute(tail, axis, [(i, (i + 1) % count) for i in range(count)])  26.1 us
    dot_general x31, matrix products, turn(): return jnp.dot(before, coarse_prop, precision=lax.Precision.HIGHEST) + flat  22 us
    add x7, other arithmetic, advance(): field + coupling * (stream + beside_y + beside_z) - damping * field  20.1 us
  transfers between devices with their start and end apart: 49, of which 41 were waited for; matrix products, arithmetic and copies ran while one was open for 0% of the time, Pallas kernels for 0%

commit v1 on v0

v1 whole, which is shorter than its diff:
```python
import functools

import jax
import jax.numpy as jnp
from jax import lax
from jax.experimental import pallas as pl
from jax.experimental.pallas import tpu as pltpu
from jax.sharding import PartitionSpec as P

MESH = pl.DeviceIdType.MESH
COUPLING = 0.12
F32, BF16 = jnp.float32, jnp.bfloat16
NT, NS = 32, 16
X, Y, Z = 16, 8, 512
H = 8
PAD = 4
LOWER, UPPER = 0, 1


def split(value):
    high = value.astype(BF16)
    return high, (value - high.astype(F32)).astype(BF16)


def product(value, high, low):
    first, second = split(value)
    return (
        jnp.dot(first, high, preferred_element_type=F32)
        + jnp.dot(first, low, preferred_element_type=F32)
        + jnp.dot(second, high, preferred_element_type=F32)
    )


def kernel(
    initial, stale, guess, forcing, classes, table, coarse,
    landed, norm,
    levels, force, walls, keep, prop, high, low, outbox, scan, result, beside, partial, gathered,
    local_sem, halo_send, halo_recv, turn_send, turn_recv, back_send, back_recv, own_sem,
    beside_send, beside_recv, norm_send, norm_recv,
):
    tm, sp = lax.axis_index("tm"), lax.axis_index("space")
    up, down = (sp + 1) & (NS - 1), (sp + NS - 1) & (NS - 1)
    last, head = tm == NT - 1, tm == NT - 2

    barrier = pltpu.get_barrier_semaphore()

    def greet(peer, slab):
        pl.semaphore_signal(barrier, inc=1, device_id=(peer, slab), device_id_type=MESH)

    greet(tm, up)
    greet(tm, down)
    for i in range(1, NT):
        greet((tm + i) & (NT - 1), sp)
    for i in range(1, NS):
        greet((tm + NT - 2) & (NT - 1), (sp + i) & (NS - 1))

    own = pl.ds(H, X)
    loads = [
        pltpu.make_async_copy(forcing, force.at[own], local_sem.at[1]),
        pltpu.make_async_copy(classes, walls.at[own], local_sem.at[2]),
        pltpu.make_async_copy(coarse, prop, local_sem.at[3]),
    ]
    field = pltpu.make_async_copy(guess.at[0], levels.at[0, own], local_sem.at[0])

    @pl.when(last)
    def _():
        pltpu.make_async_copy(stale, levels.at[0, own], local_sem.at[0]).start()

    @pl.when(jnp.logical_not(last))
    def _():
        field.start()

    for copy in loads:
        copy.start()
    pltpu.make_async_copy(initial, levels.at[9, own], local_sem.at[4]).start()

    pl.semaphore_wait(barrier, 2 + NT - 1 + NS - 1)

    def halo(source, target, side, index, rows):
        if side == 0:
            here, there, slab = pl.ds(X - rows, rows), pl.ds(H - rows, rows), up
        else:
            here, there, slab = pl.ds(0, rows), pl.ds(H + X, rows), down
        return pltpu.make_async_remote_copy(
            src_ref=source.at[here], dst_ref=target.at[there],
            send_sem=halo_send.at[side, index], recv_sem=halo_recv.at[side, index],
            device_id=(tm, slab), device_id_type=MESH,
        )

    sides = (1, 0)
    for side in sides:
        @pl.when(last)
        def _():
            halo(stale, levels.at[0], side, 0, 8).start()

        @pl.when(jnp.logical_not(last))
        def _():
            halo(guess.at[0], levels.at[0], side, 0, 8).start()

        halo(forcing, force, side, 1, 7).start()
        halo(classes, walls, side, 2, 7).start()

        @pl.when(head)
        def _():
            halo(initial, levels.at[9], side, 3, 4).start()

    loads[2].wait()

    def keep_split(power, rows, value):
        first, second = split(value)
        high[power, rows, :] = first
        low[power, rows, :] = second

    def start_power(i, carry):
        rows = pl.ds(pl.multiple_of(i * 128, 128), 128)
        keep_split(0, rows, prop[rows, :])
        return carry

    lax.fori_loop(0, Z // 128, start_power, 0)
    for power in range(1, 4):
        def square(i, carry):
            rows = pl.ds(pl.multiple_of(i * 128, 128), 128)
            first, second = high[power - 1, rows, :], low[power - 1, rows, :]
            value = (
                jnp.dot(first, high[power - 1], preferred_element_type=F32)
                + jnp.dot(first, low[power - 1], preferred_element_type=F32)
                + jnp.dot(second, high[power - 1], preferred_element_type=F32)
            )
            keep_split(power, rows, value)
            return carry

        lax.fori_loop(0, Z // 128, square, 0)

    lane = lax.broadcasted_iota(jnp.int32, (1, Y, Z), 2)
    row = lax.broadcasted_iota(jnp.int32, (1, Y, Z), 1)
    not_left, not_right = lane > 0, lane < Z - 1
    not_first, not_final = row > 0, row < Y - 1

    def keep_factor(start, count):
        def one(i, carry):
            wall = walls[start + i]
            damping = jnp.zeros((Y, Z), F32)
            for class_no in range(4):
                damping = jnp.where(wall == class_no, table[class_no], damping)
            keep[start + i] = (1.0 - 6.0 * COUPLING) - damping
            return carry

        lax.fori_loop(0, count, one, 0)

    second_source = jnp.where(head, 9, 4)

    def step(level, start, count):
        source = second_source if level == 5 else level - 1

        def rows(at, size):
            field = levels[source, pl.ds(at, size)]
            around = levels[source, pl.ds(at - 1, size)] + levels[source, pl.ds(at + 1, size)]
            around += jnp.where(not_left, pltpu.roll(field, 1, 2), 0.0)
            around += jnp.where(not_right, pltpu.roll(field, Z - 1, 2), 0.0)
            around += jnp.where(not_first, pltpu.roll(field, 1, 1), 0.0)
            around += jnp.where(not_final, pltpu.roll(field, Y - 1, 1), 0.0)
            levels[level, pl.ds(at, size)] = (
                field * keep[pl.ds(at, size)] + COUPLING * around + force[pl.ds(at, size)]
            )

        pair = 2

        def one(i, carry):
            rows(start + i * pair, pair)
            return carry

        lax.fori_loop(0, count // pair, one, 0)

    def wait_halo(side):
        for index, (buffer, count) in enumerate(((levels.at[0], 8), (force, 7), (walls, 7))):
            there = pl.ds(H - count, count) if side == 0 else pl.ds(H + X, count)
            pltpu.make_async_copy(buffer.at[there], buffer.at[there], halo_recv.at[side, index]).wait()

        @pl.when(head)
        def _():
            there = pl.ds(H - 4, 4) if side == 0 else pl.ds(H + X, 4)
            pltpu.make_async_copy(levels.at[9, there], levels.at[9, there], halo_recv.at[side, 3]).wait()

    def half_rows(half):
        return pl.ds(H + half * 8, 8)

    def send_half(half):
        pltpu.make_async_remote_copy(
            src_ref=levels.at[4, half_rows(half)], dst_ref=beside.at[half],
            send_sem=beside_send.at[half], recv_sem=beside_recv.at[half],
            device_id=((tm + NT - 1) & (NT - 1), sp), device_id_type=MESH,
        ).start()
        relaxed = levels[4, half_rows(half)].reshape(64, Z)
        carried = product(relaxed, high[0], low[0]).reshape(8, Y, Z)
        term = levels[8, half_rows(half)] - jnp.where(head, 0.0, carried)
        for x in range(8):
            for k in range(4):
                outbox[half, pl.ds(x * 32 + k, 8, stride=4), :] = term[x, :, k * 128 : (k + 1) * 128]
        place = (tm + 2) & (NT - 1)
        pltpu.make_async_copy(
            outbox.at[half, pl.ds(pl.multiple_of(tm * 8, 8), 8)],
            scan.at[half, 0, pl.ds(pl.multiple_of((place + PAD) * 8, 8), 8)],
            own_sem.at[half, 0],
        ).start()
        for i in range(1, NT):
            peer = (tm + i) & (NT - 1)
            pltpu.make_async_remote_copy(
                src_ref=outbox.at[half, pl.ds(pl.multiple_of(peer * 8, 8), 8)],
                dst_ref=scan.at[half, 0, pl.ds(pl.multiple_of((place + PAD) * 8, 8), 8)],
                send_sem=turn_send.at[half], recv_sem=turn_recv.at[half],
                device_id=(peer, sp), device_id_type=MESH,
            ).start()

    for copy in (field, *loads[:2]):
        copy.wait()
    pltpu.make_async_copy(initial, levels.at[9, own], local_sem.at[4]).wait()
    for half in range(2):
        for stage in range(3):
            scan[half, stage, 0 : PAD * 8, :] = jnp.zeros((PAD * 8, 128), F32)
    keep_factor(H, X)
    for level in range(1, 8):
        step(level, H + level, X - 2 * level)
    wait_halo(1)
    keep_factor(H + X, 7)
    for level in range(1, 9):
        step(level, H + X - level, 8)
    send_half(UPPER)
    wait_halo(0)
    keep_factor(1, 7)
    for level in range(1, 9):
        step(level, level, 8)
    send_half(LOWER)

    total = jnp.zeros((Y, Z), F32)
    for half in (UPPER, LOWER):
        pltpu.make_async_copy(beside.at[half], beside.at[half], beside_recv.at[half]).wait()

        def add(i, sums):
            residual = levels[8, H + half * 8 + i] - beside[half, i]
            return sums + residual * residual

        total = lax.fori_loop(0, 8, add, total)
    lanes = total[:, 0:128] + total[:, 128:256] + total[:, 256:384] + total[:, 384:512]
    partial[...] = jnp.sum(lanes, axis=0, keepdims=True)
    for i in range(NS):
        pltpu.make_async_remote_copy(
            src_ref=partial, dst_ref=gathered.at[sp], send_sem=norm_send, recv_sem=norm_recv,
            device_id=((tm + 2) & (NT - 1), (sp + i) & (NS - 1)), device_id_type=MESH,
        ).start()

    def view(half, stage, first, slices):
        pieces = [
            scan[half, stage, pl.ds(first * 8 + k, slices * 2, stride=4), :] for k in range(4)
        ]
        return jnp.concatenate(pieces, axis=1)

    def store(buffer, first, slices, value):
        for k in range(4):
            buffer[pl.ds(first * 8 + k, slices * 2, stride=4), :] = value[:, k * 128 : (k + 1) * 128]

    for half in (UPPER, LOWER):
        mine = outbox.at[half, pl.ds(0, 8)]
        pltpu.make_async_copy(mine, mine, own_sem.at[half, 0]).wait()
        others = outbox.at[half, pl.ds(0, (NT - 1) * 8)]
        pltpu.make_async_copy(others, others, turn_recv.at[half]).wait()
        for stage in range(3):
            after = view(half, stage, PAD, NT) + product(
                view(half, stage, PAD - (1 << stage), NT), high[stage], low[stage]
            )
            if stage < 2:
                store(scan.at[half, stage + 1], PAD, NT, after)
        chunk = after[0:16]
        chunks = [chunk]
        for c in range(1, 4):
            chunk = after[c * 16 : (c + 1) * 16] + product(chunk, high[3], low[3])
            chunks.append(chunk)
        store(result.at[half], 0, NT, jnp.concatenate(chunks, axis=0))
        here = landed.at[pl.ds(pl.multiple_of(half * 256 + tm * 8, 8), 8)]
        pltpu.make_async_copy(
            result.at[half, pl.ds(pl.multiple_of(tm * 8, 8), 8)], here, own_sem.at[half, 1]
        ).start()
        for i in range(1, NT):
            peer = (tm + i) & (NT - 1)
            pltpu.make_async_remote_copy(
                src_ref=result.at[half, pl.ds(pl.multiple_of(peer * 8, 8), 8)], dst_ref=here,
                send_sem=back_send.at[half], recv_sem=back_recv.at[half],
                device_id=(peer, sp), device_id_type=MESH,
            ).start()

    pltpu.make_async_copy(gathered, gathered, norm_recv).wait()
    squares = jnp.sum(gathered[...], axis=0)
    mean = jnp.sum(squares, axis=1, keepdims=True) / (NS * X * Y * Z)
    norm[...] = jnp.broadcast_to(jnp.sqrt(mean), (8, 128))

    for half in range(2):
        mine = outbox.at[half, pl.ds(0, 8)]
        others = outbox.at[half, pl.ds(0, (NT - 1) * 8)]
        pltpu.make_async_copy(mine, mine, own_sem.at[half, 1]).wait()
        pltpu.make_async_copy(others, others, back_recv.at[half]).wait()
        pltpu.make_async_copy(others, others, turn_send.at[half]).wait()
        pltpu.make_async_copy(others, others, back_send.at[half]).wait()
        pltpu.make_async_copy(beside.at[half], beside.at[half], beside_send.at[half]).wait()
    pltpu.make_async_copy(gathered, gathered, norm_send).wait()
    for side in sides:
        for index, (buffer, count) in enumerate(((levels.at[0], 8), (force, 7), (walls, 7))):
            there = pl.ds(0, count)
            pltpu.make_async_copy(buffer.at[there], buffer.at[there], halo_send.at[side, index]).wait()

        @pl.when(head)
        def _():
            there = pl.ds(0, 4)
            pltpu.make_async_copy(levels.at[9, there], levels.at[9, there], halo_send.at[side, 3]).wait()


def shards(initial, stale_start, guess, forcing, wall_class, damping_table, coarse_prop):
    anywhere = pl.BlockSpec(memory_space=pl.ANY)
    dma = pltpu.SemaphoreType.DMA
    landed, norm = pl.pallas_call(
        kernel,
        out_shape=(
            jax.ShapeDtypeStruct((X * Y * Z // 128, 128), F32),
            jax.ShapeDtypeStruct((8, 128), F32),
        ),
        in_specs=[anywhere] * 5 + [pl.BlockSpec(memory_space=pltpu.SMEM), anywhere],
        out_specs=(anywhere, pl.BlockSpec(memory_space=pltpu.VMEM)),
        scratch_shapes=[
            pltpu.VMEM((10, X + 2 * H, Y, Z), F32),
            pltpu.VMEM((X + 2 * H, Y, Z), F32),
            pltpu.VMEM((X + 2 * H, Y, Z), jnp.int32),
            pltpu.VMEM((X + 2 * H, Y, Z), F32),
            pltpu.VMEM((Z, Z), F32),
            pltpu.VMEM((4, Z, Z), BF16),
            pltpu.VMEM((4, Z, Z), BF16),
            pltpu.VMEM((2, NT * 8, 128), F32),
            pltpu.VMEM((2, 3, (PAD + NT) * 8, 128), F32),
            pltpu.VMEM((2, NT * 8, 128), F32),
            pltpu.VMEM((2, 8, Y, Z), F32),
            pltpu.VMEM((1, 128), F32),
            pltpu.VMEM((NS, 1, 128), F32),
            dma((5,)), dma((2, 4)), dma((2, 4)), dma((2,)), dma((2,)), dma((2,)), dma((2,)),
            dma((2, 2)), dma((2,)), dma((2,)), dma, dma,
        ],
        compiler_params=pltpu.CompilerParams(
            collective_id=0, has_side_effects=True, vmem_limit_bytes=48 * 1024 * 1024
        ),
    )(initial, stale_start, guess, forcing, wall_class, damping_table, coarse_prop)
    return landed.reshape(1, X, Y, Z), norm[0, 0:1]


def solution(mesh):
    return jax.shard_map(
        shards,
        mesh=mesh,
        in_specs=(
            P("space", None, None),
            P("space", None, None),
            P("tm", "space", None, None),
            P("space", None, None),
            P("space", None, None),
            P(),
            P(),
        ),
        out_specs=(P("tm", "space", None, None), P("tm")),
        check_vma=False,
    )
```

time: 485 us -> 57.9 us (0.12)
  the two profiles are of different devices: /device:TPU:24 before, /device:TPU:1 now
where the time goes in v1:
time: 57.9 us; the launch traced here: 57.6 us
  Pallas kernels  49 us (85%)
  local copies, waits for them, and re-layouts  7.88 us (14%)
  between operations  0.66 us (1%)
    pallas_call x1, Pallas kernels, shards(): pl.pallas_call(kernel, out_shape=(jax.ShapeDtypeStruct((X * Y * Z // 128,...  49 us
    unnamed x14, local copies, waits for them, and re-layouts  6.62 us

profile of v1, /device:TPU:1, one launch (start us, length us, event | category | flops | bytes accessed | tf_op | source)
XLA Modules:
  0.0 57.6 jit_solution(6775071464835370985)
XLA Ops:
  0.6 0.0 copy-start
  0.6 1.2 %copy-done = f32[512,512]{1,0:T(8,128)S(1)} copy-done((f32[512,512]{1,0:T(8,128)S(1)}, f32[512,512]{1,0:T(8,128)}, u32[]{:S(2)}) %copy-start) | copy-done | bytes 1048600
  1.9 0.0 copy-start.1
  1.9 0.9 %copy-done.1 = f32[16,8,512]{2,1,0:T(8,128)S(1)} copy-done((f32[16,8,512]{2,1,0:T(8,128)S(1)}, f32[16,8,512]{2,1,0:T(8,128)}, u32[]{:S(2)}) %copy-start.1) | copy-done | bytes 262168
  2.8 0.0 copy-start.2
  2.8 0.9 %copy-done.2 = f32[16,8,512]{2,1,0:T(8,128)S(1)} copy-done((f32[16,8,512]{2,1,0:T(8,128)S(1)}, f32[16,8,512]{2,1,0:T(8,128)}, u32[]{:S(2)}) %copy-start.2) | copy-done | bytes 262168
  3.8 0.0 copy-start.3
  3.8 0.9 %copy-done.3 = f32[1,16,8,512]{3,2,1,0:T(8,128)S(1)} copy-done((f32[1,16,8,512]{3,2,1,0:T(8,128)S(1)}, f32[1,16,8,512]{3,2,1,0:T(8,128)}, u32[]{:S(2)}) %copy-start.3) | copy-done | bytes 262168
  4.7 0.0 copy-start.4
  4.7 0.9 %copy-done.4 = f32[16,8,512]{2,1,0:T(8,128)S(1)} copy-done((f32[16,8,512]{2,1,0:T(8,128)S(1)}, f32[16,8,512]{2,1,0:T(8,128)}, u32[]{:S(2)}) %copy-start.4) | copy-done | bytes 262168
  5.7 0.0 copy-start.5
  5.7 0.9 %copy-done.5 = s32[16,8,512]{2,1,0:T(8,128)S(1)} copy-done((s32[16,8,512]{2,1,0:T(8,128)S(1)}, s32[16,8,512]{2,1,0:T(8,128)}, u32[]{:S(2)}) %copy-start.5) | copy-done | bytes 262168
  6.6 0.0 copy-start.6
  6.6 0.7 %copy-done.6 = f32[4]{0:T(128)S(1)} copy-done((f32[4]{0:T(128)S(1)}, f32[4]{0:T(128)}, u32[]{:S(2)}) %copy-start.6) | copy-done | bytes 40
  7.3 49.0 %shard_map.86 = (f32[512,128]{1,0:T(8,128)S(1)}, f32[8,128]{1,0:T(8,128)S(1)}) custom-call(f32[16,8,512]{2,1,0:T(8,128)S(1)} %copy-done.1, f32[16,8,512]{2,1,0:T(8,128)S(1)} %copy-done.2, f32[1,16,8,512]{3,2,1,0:T(8,128)S(1)} %copy-done.3, f32[16,8,512]{2,1,0:T(8,128)S(1)} %copy-done.4, s32[16,8,512]{2,1,0:T(8,128)S(1)} %copy-done.5, f32[4]{0:T(128)S(1)} %copy-done.6, ...), custom_call_target="tpu_custom_call" | custom-call | tf_op jit(solution)/shard_map/pallas_call | solution.py:318
  56.3 0.5 slice.3
  56.8 0.7 %reshape.7 = f32[1,16,8,512]{3,2,1,0:T(8,128)} reshape(f32[512,128]{1,0:T(8,128)S(1)} %get-tuple-element.4) | data formatting | bytes 524288 | tf_op jit(solution)/shard_map/reshape | solution.py:347
Async XLA Ops:
  0.6 1.2 %copy-start = (f32[512,512]{1,0:T(8,128)S(1)}, f32[512,512]{1,0:T(8,128)}, u32[]{:S(2)}) copy-start(f32[512,512]{1,0:T(8,128)} %coarse.1) | copy-start | bytes 3145732
  1.9 0.9 %copy-start.1 = (f32[16,8,512]{2,1,0:T(8,128)S(1)}, f32[16,8,512]{2,1,0:T(8,128)}, u32[]{:S(2)}) copy-start(f32[16,8,512]{2,1,0:T(8,128)} %initial.1) | copy-start | bytes 786436
  2.8 0.9 %copy-start.2 = (f32[16,8,512]{2,1,0:T(8,128)S(1)}, f32[16,8,512]{2,1,0:T(8,128)}, u32[]{:S(2)}) copy-start(f32[16,8,512]{2,1,0:T(8,128)} %stale.1) | copy-start | bytes 786436
  3.8 0.9 %copy-start.3 = (f32[1,16,8,512]{3,2,1,0:T(8,128)S(1)}, f32[1,16,8,512]{3,2,1,0:T(8,128)}, u32[]{:S(2)}) copy-start(f32[1,16,8,512]{3,2,1,0:T(8,128)} %guess.1) | copy-start | bytes 786436
  4.7 0.9 %copy-start.4 = (f32[16,8,512]{2,1,0:T(8,128)S(1)}, f32[16,8,512]{2,1,0:T(8,128)}, u32[]{:S(2)}) copy-start(f32[16,8,512]{2,1,0:T(8,128)} %forcing.1) | copy-start | bytes 786436
  5.7 0.9 %copy-start.5 = (s32[16,8,512]{2,1,0:T(8,128)S(1)}, s32[16,8,512]{2,1,0:T(8,128)}, u32[]{:S(2)}) copy-start(s32[16,8,512]{2,1,0:T(8,128)} %classes.1) | copy-start | bytes 786436
  6.6 0.7 %copy-start.6 = (f32[4]{0:T(128)S(1)}, f32[4]{0:T(128)}, u32[]{:S(2)}) copy-start(f32[4]{0:T(128)} %table.1) | copy-start | bytes 52

commit v2 on v1

--- a/solution.py
+++ b/solution.py
@@ -32,11 +32,11 @@
 
 
 def kernel(
-    initial, stale, guess, forcing, classes, table, coarse,
+    initial, stale, guess, forcing, classes, damping_table, coarse,
     landed, norm,
-    levels, force, walls, keep, prop, high, low, outbox, scan, result, beside, partial, gathered,
+    table, levels, force, walls, keep, prop, high, low, outbox, scan, result, beside, partial, gathered,
     local_sem, halo_send, halo_recv, turn_send, turn_recv, back_send, back_recv, own_sem,
-    beside_send, beside_recv, norm_send, norm_recv,
+    beside_send, beside_recv, norm_send, norm_recv, known,
 ):
     tm, sp = lax.axis_index("tm"), lax.axis_index("space")
     up, down = (sp + 1) & (NS - 1), (sp + NS - 1) & (NS - 1)
@@ -51,8 +51,6 @@
     greet(tm, down)
     for i in range(1, NT):
         greet((tm + i) & (NT - 1), sp)
-    for i in range(1, NS):
-        greet((tm + NT - 2) & (NT - 1), (sp + i) & (NS - 1))
 
     own = pl.ds(H, X)
     loads = [
@@ -70,11 +68,23 @@
     def _():
         field.start()
 
+    copy_table = pltpu.make_async_copy(damping_table, table, local_sem.at[5])
+    copy_table.start()
     for copy in loads:
         copy.start()
     pltpu.make_async_copy(initial, levels.at[9, own], local_sem.at[4]).start()
 
-    pl.semaphore_wait(barrier, 2 + NT - 1 + NS - 1)
+    pl.semaphore_wait(barrier, 2 + NT - 1)
+
+    def tell(round_no):
+        for way in (1, -1)[: 1 if round_no == 3 else 2]:
+            pl.semaphore_signal(
+                known.at[round_no], inc=1,
+                device_id=(tm, (sp + NS + (way << round_no)) & (NS - 1)), device_id_type=MESH,
+            )
+
+    def hear(round_no):
+        pl.semaphore_wait(known.at[round_no], 1 if round_no == 3 else 2)
 
     def halo(source, target, side, index, rows):
         if side == 0:
@@ -103,6 +113,8 @@
         @pl.when(head)
         def _():
             halo(initial, levels.at[9], side, 3, 4).start()
+
+    tell(0)
 
     loads[2].wait()
 
@@ -163,13 +175,8 @@
                 field * keep[pl.ds(at, size)] + COUPLING * around + force[pl.ds(at, size)]
             )
 
-        pair = 2
-
-        def one(i, carry):
-            rows(start + i * pair, pair)
-            return carry
-
-        lax.fori_loop(0, count // pair, one, 0)
+        for i in range(0, count, 4):
+            rows(start + i, min(4, count - i))
 
     def wait_halo(side):
         for index, (buffer, count) in enumerate(((levels.at[0], 8), (force, 7), (walls, 7))):
@@ -211,7 +218,7 @@
                 device_id=(peer, sp), device_id_type=MESH,
             ).start()
 
-    for copy in (field, *loads[:2]):
+    for copy in (copy_table, field, *loads[:2]):
         copy.wait()
     pltpu.make_async_copy(initial, levels.at[9, own], local_sem.at[4]).wait()
     for half in range(2):
@@ -220,16 +227,22 @@
     keep_factor(H, X)
     for level in range(1, 8):
         step(level, H + level, X - 2 * level)
+    hear(0)
+    tell(1)
     wait_halo(1)
     keep_factor(H + X, 7)
     for level in range(1, 9):
         step(level, H + X - level, 8)
     send_half(UPPER)
+    hear(1)
+    tell(2)
     wait_halo(0)
     keep_factor(1, 7)
     for level in range(1, 9):
         step(level, level, 8)
     send_half(LOWER)
+    hear(2)
+    tell(3)
 
     total = jnp.zeros((Y, Z), F32)
     for half in (UPPER, LOWER):
@@ -242,6 +255,7 @@
         total = lax.fori_loop(0, 8, add, total)
     lanes = total[:, 0:128] + total[:, 128:256] + total[:, 256:384] + total[:, 384:512]
     partial[...] = jnp.sum(lanes, axis=0, keepdims=True)
+    hear(3)
     for i in range(NS):
         pltpu.make_async_remote_copy(
             src_ref=partial, dst_ref=gathered.at[sp], send_sem=norm_send, recv_sem=norm_recv,
@@ -314,6 +328,7 @@
 
 def shards(initial, stale_start, guess, forcing, wall_class, damping_table, coarse_prop):
     anywhere = pl.BlockSpec(memory_space=pl.ANY)
+    hbm = pl.BlockSpec(memory_space=pltpu.HBM)
     dma = pltpu.SemaphoreType.DMA
     landed, norm = pl.pallas_call(
         kernel,
@@ -321,9 +336,10 @@
             jax.ShapeDtypeStruct((X * Y * Z // 128, 128), F32),
             jax.ShapeDtypeStruct((8, 128), F32),
         ),
-        in_specs=[anywhere] * 5 + [pl.BlockSpec(memory_space=pltpu.SMEM), anywhere],
+        in_specs=[hbm] * 7,
         out_specs=(anywhere, pl.BlockSpec(memory_space=pltpu.VMEM)),
         scratch_shapes=[
+            pltpu.SMEM((4,), F32),
             pltpu.VMEM((10, X + 2 * H, Y, Z), F32),
             pltpu.VMEM((X + 2 * H, Y, Z), F32),
             pltpu.VMEM((X + 2 * H, Y, Z), jnp.int32),
@@ -337,11 +353,11 @@
             pltpu.VMEM((2, 8, Y, Z), F32),
             pltpu.VMEM((1, 128), F32),
             pltpu.VMEM((NS, 1, 128), F32),
-            dma((5,)), dma((2, 4)), dma((2, 4)), dma((2,)), dma((2,)), dma((2,)), dma((2,)),
-            dma((2, 2)), dma((2,)), dma((2,)), dma, dma,
+            dma((6,)), dma((2, 4)), dma((2, 4)), dma((2,)), dma((2,)), dma((2,)), dma((2,)),
+            dma((2, 2)), dma((2,)), dma((2,)), dma, dma, pltpu.SemaphoreType.REGULAR((4,)),
         ],
         compiler_params=pltpu.CompilerParams(
-            collective_id=0, has_side_effects=True, vmem_limit_bytes=48 * 1024 * 1024
+            collective_id=0, has_side_effects=True, vmem_limit_bytes=63 * 1024 * 1024
         ),
     )(initial, stale_start, guess, forcing, wall_class, damping_table, coarse_prop)
     return landed.reshape(1, X, Y, Z), norm[0, 0:1]

time: 57.9 us -> 48.4 us (0.84)
  local copies, waits for them, and re-layouts: 7.88 us -> 2.89 us
  Pallas kernels: 49 us -> 44.7 us
    unnamed x14 -> x0, local copies, waits for them, and re-layouts: 6.62 us -> none
    pallas_call x1, Pallas kernels: 49 us -> 44.7 us  [shards(): pl.pallas_call(kernel, out_shape=(jax.ShapeDtypeStruct((X * Y * Z // 128,...]
    reshape x1, local copies, waits for them, and re-layouts: 0.74 us -> 1.69 us  [shards(): return (landed.reshape(1, X, Y, Z), norm[0, 0:1])]
    slice x1, local copies, waits for them, and re-layouts: 0.51 us -> 1.2 us  [shards(): return (landed.reshape(1, X, Y, Z), norm[0, 0:1])]
where the time goes in v2:
time: 48.4 us; the launch traced here: 48.3 us
  Pallas kernels  44.7 us (92%)
  local copies, waits for them, and re-layouts  2.89 us (6%)
  between operations  0.64 us (1%)
    pallas_call x1, Pallas kernels, shards(): pl.pallas_call(kernel, out_shape=(jax.ShapeDtypeStruct((X * Y * Z // 128,...  44.7 us
    reshape x1, local copies, waits for them, and re-layouts, shards(): return (landed.reshape(1, X, Y, Z), norm[0, 0:1])  1.69 us
    slice x1, local copies, waits for them, and re-layouts, shards(): return (landed.reshape(1, X, Y, Z), norm[0, 0:1])  1.2 us

profile of v2, /device:TPU:1, one launch (start us, length us, event | category | flops | bytes accessed | tf_op | source)
XLA Modules:
  0.0 48.3 jit_solution(10725837982269256572)
XLA Ops:
  0.6 44.7 %shard_map.86 = (f32[512,128]{1,0:T(8,128)}, f32[8,128]{1,0:T(8,128)}) custom-call(f32[16,8,512]{2,1,0:T(8,128)} %initial.1, f32[16,8,512]{2,1,0:T(8,128)} %stale.1, f32[1,16,8,512]{3,2,1,0:T(8,128)} %guess.1, f32[16,8,512]{2,1,0:T(8,128)} %forcing.1, s32[16,8,512]{2,1,0:T(8,128)} %classes.1, f32[4]{0:T(128)} %damping_table.1, f32[512,512]{1,0:T(8,128)} %coarse.1), custom_call_target="tpu_custom_call" | custom-call | tf_op jit(solution)/shard_map/pallas_call | solution.py:333
  45.4 1.2 %slice.3 = f32[1,1]{1,0:T(1,128)} slice(f32[8,128]{1,0:T(8,128)} %get-tuple-element.5), slice={[0:1], [0:1]} | slice | bytes 8 | tf_op jit(solution)/shard_map/slice | solution.py:363
  46.6 1.7 %reshape.7 = f32[1,16,8,512]{3,2,1,0:T(8,128)} reshape(f32[512,128]{1,0:T(8,128)} %get-tuple-element.4) | data formatting | bytes 524288 | tf_op jit(solution)/shard_map/reshape | solution.py:363

commit v3 on v2

--- a/solution.py
+++ b/solution.py
@@ -12,8 +12,10 @@
 F32, BF16 = jnp.float32, jnp.bfloat16
 NT, NS = 32, 16
 X, Y, Z = 16, 8, 512
+MIDDLE = 4
 H = 8
 PAD = 4
+BLOCK = 256
 LOWER, UPPER = 0, 1
 
 
@@ -29,6 +31,18 @@
         + jnp.dot(first, low, preferred_element_type=F32)
         + jnp.dot(second, high, preferred_element_type=F32)
     )
+
+
+def moved(tm, dy, dx, dc):
+    return ((tm + 8 * dy) & 24) | ((tm + 2 * dx) & 6) | ((tm ^ dc) & 1)
+
+
+PEERS = sorted(
+    [(dy, dx, dc) for dy in range(4) for dx in range(4) for dc in range(2)][1:],
+    key=lambda d: -min(d[0], 4 - d[0]) - min(d[1], 4 - d[1]),
+)
+LINE = [(0, dx, dc) for dx in range(4) for dc in range(2)][1:]
+BESIDE = LINE + [(dy, 0, dc) for dy in range(1, 4) for dc in range(2)]
 
 
 def kernel(
@@ -49,8 +63,15 @@
 
     greet(tm, up)
     greet(tm, down)
-    for i in range(1, NT):
-        greet((tm + i) & (NT - 1), sp)
+    for move in BESIDE:
+        greet(moved(tm, *move), sp)
+    middle = sp == MIDDLE
+
+    @pl.when(middle)
+    def _():
+        for i in range(2, NS - 1):
+            greet(tm, MIDDLE + i & (NS - 1))
+
 
     own = pl.ds(H, X)
     loads = [
@@ -60,31 +81,67 @@
     ]
     field = pltpu.make_async_copy(guess.at[0], levels.at[0, own], local_sem.at[0])
 
-    @pl.when(last)
-    def _():
-        pltpu.make_async_copy(stale, levels.at[0, own], local_sem.at[0]).start()
-
-    @pl.when(jnp.logical_not(last))
-    def _():
-        field.start()
-
     copy_table = pltpu.make_async_copy(damping_table, table, local_sem.at[5])
-    copy_table.start()
-    for copy in loads:
-        copy.start()
-    pltpu.make_async_copy(initial, levels.at[9, own], local_sem.at[4]).start()
-
-    pl.semaphore_wait(barrier, 2 + NT - 1)
-
-    def tell(round_no):
-        for way in (1, -1)[: 1 if round_no == 3 else 2]:
-            pl.semaphore_signal(
-                known.at[round_no], inc=1,
-                device_id=(tm, (sp + NS + (way << round_no)) & (NS - 1)), device_id_type=MESH,
-            )
-
-    def hear(round_no):
-        pl.semaphore_wait(known.at[round_no], 1 if round_no == 3 else 2)
+
+    def load():
+        copy_table.start()
+        for copy in loads:
+            copy.start()
+        pltpu.make_async_copy(initial, levels.at[9, own], local_sem.at[4]).start()
+
+        @pl.when(last)
+        def _():
+            pltpu.make_async_copy(stale, levels.at[0, own], local_sem.at[0]).start()
+
+        @pl.when(jnp.logical_not(last))
+        def _():
+            field.start()
+
+    def keep_split(power, rows, value):
+        first, second = split(value)
+        high[power, rows, :] = first
+        low[power, rows, :] = second
+
+    def split_prop():
+        loads[2].wait()
+
+        def one(i, carry):
+            rows = pl.ds(pl.multiple_of(i * 128, 128), 128)
+            keep_split(0, rows, prop[rows, :])
+            return carry
+
+        lax.fori_loop(0, Z // 128, one, 0)
+
+    def powers():
+        for power in range(1, 4):
+            def square(i, carry):
+                rows = pl.ds(pl.multiple_of(i * BLOCK, BLOCK), BLOCK)
+                first, second = high[power - 1, rows, :], low[power - 1, rows, :]
+                value = (
+                    jnp.dot(first, high[power - 1], preferred_element_type=F32)
+                    + jnp.dot(first, low[power - 1], preferred_element_type=F32)
+                    + jnp.dot(second, high[power - 1], preferred_element_type=F32)
+                )
+                keep_split(power, rows, value)
+                return carry
+
+            lax.fori_loop(0, Z // BLOCK, square, 0)
+
+    early = sp < NS // 2
+
+    @pl.when(early)
+    def _():
+        load()
+        split_prop()
+        powers()
+
+    beside_middle = (sp >= MIDDLE - 1) & (sp <= MIDDLE + 1)
+    pl.semaphore_wait(barrier, 2 + len(BESIDE) + jnp.where(beside_middle, 0, 1))
+
+    def tell(index, slices, slabs):
+        for peer in slices:
+            for slab in slabs:
+                pl.semaphore_signal(known.at[index], inc=1, device_id=(peer, slab), device_id_type=MESH)
 
     def halo(source, target, side, index, rows):
         if side == 0:
@@ -97,8 +154,18 @@
             device_id=(tm, slab), device_id_type=MESH,
         )
 
-    sides = (1, 0)
+    core = tm & 1
+    other = tm ^ 1
+    sides = (0, 1)
     for side in sides:
+        @pl.when(core == 0)
+        def _():
+            halo(forcing, force, side, 1, 7).start()
+
+        @pl.when(core == 1)
+        def _():
+            halo(classes, walls, side, 1, 7).start()
+
         @pl.when(last)
         def _():
             halo(stale, levels.at[0], side, 0, 8).start()
@@ -107,41 +174,25 @@
         def _():
             halo(guess.at[0], levels.at[0], side, 0, 8).start()
 
-        halo(forcing, force, side, 1, 7).start()
-        halo(classes, walls, side, 2, 7).start()
-
         @pl.when(head)
         def _():
             halo(initial, levels.at[9], side, 3, 4).start()
 
-    tell(0)
-
-    loads[2].wait()
-
-    def keep_split(power, rows, value):
-        first, second = split(value)
-        high[power, rows, :] = first
-        low[power, rows, :] = second
-
-    def start_power(i, carry):
-        rows = pl.ds(pl.multiple_of(i * 128, 128), 128)
-        keep_split(0, rows, prop[rows, :])
-        return carry
-
-    lax.fori_loop(0, Z // 128, start_power, 0)
-    for power in range(1, 4):
-        def square(i, carry):
-            rows = pl.ds(pl.multiple_of(i * 128, 128), 128)
-            first, second = high[power - 1, rows, :], low[power - 1, rows, :]
-            value = (
-                jnp.dot(first, high[power - 1], preferred_element_type=F32)
-                + jnp.dot(first, low[power - 1], preferred_element_type=F32)
-                + jnp.dot(second, high[power - 1], preferred_element_type=F32)
-            )
-            keep_split(power, rows, value)
-            return carry
-
-        lax.fori_loop(0, Z // 128, square, 0)
+    tell(0, [moved(tm, *move) for move in LINE], [sp])
+
+    @pl.when(jnp.logical_not(early))
+    def _():
+        load()
+
+    pl.semaphore_wait(known.at[0], len(LINE))
+
+    @pl.when(jnp.logical_not(middle))
+    def _():
+        tell(1, [tm], [MIDDLE])
+
+    @pl.when(jnp.logical_not(early))
+    def _():
+        split_prop()
 
     lane = lax.broadcasted_iota(jnp.int32, (1, Y, Z), 2)
     row = lax.broadcasted_iota(jnp.int32, (1, Y, Z), 1)
@@ -178,25 +229,53 @@
         for i in range(0, count, 4):
             rows(start + i, min(4, count - i))
 
+    def end(side, count):
+        return pl.ds(H - count, count) if side == 0 else pl.ds(H + X, count)
+
+    def pass_on(side):
+        there = end(side, 7)
+
+        def onward(buffer):
+            return pltpu.make_async_remote_copy(
+                src_ref=buffer.at[there], dst_ref=buffer.at[there],
+                send_sem=halo_send.at[side, 2], recv_sem=halo_recv.at[side, 2],
+                device_id=(other, sp), device_id_type=MESH,
+            )
+
+        pltpu.make_async_copy(force.at[there], force.at[there], halo_recv.at[side, 1]).wait()
+
+        @pl.when(core == 0)
+        def _():
+            onward(force).start()
+
+        @pl.when(core == 1)
+        def _():
+            onward(walls).start()
+
     def wait_halo(side):
-        for index, (buffer, count) in enumerate(((levels.at[0], 8), (force, 7), (walls, 7))):
-            there = pl.ds(H - count, count) if side == 0 else pl.ds(H + X, count)
+        for index, (buffer, count) in ((0, (levels.at[0], 8)), (2, (force, 7))):
+            there = end(side, count)
             pltpu.make_async_copy(buffer.at[there], buffer.at[there], halo_recv.at[side, index]).wait()
 
         @pl.when(head)
         def _():
-            there = pl.ds(H - 4, 4) if side == 0 else pl.ds(H + X, 4)
+            there = end(side, 4)
             pltpu.make_async_copy(levels.at[9, there], levels.at[9, there], halo_recv.at[side, 3]).wait()
 
     def half_rows(half):
         return pl.ds(H + half * 8, 8)
 
-    def send_half(half):
+    pieces = ((4, 8), (12, 4), (0, 4))
+
+    def send_relaxed(piece):
+        first, count = pieces[piece]
         pltpu.make_async_remote_copy(
-            src_ref=levels.at[4, half_rows(half)], dst_ref=beside.at[half],
-            send_sem=beside_send.at[half], recv_sem=beside_recv.at[half],
+            src_ref=levels.at[4, pl.ds(H + first, count)], dst_ref=beside.at[pl.ds(first, count)],
+            send_sem=beside_send.at[piece], recv_sem=beside_recv.at[piece],
             device_id=((tm + NT - 1) & (NT - 1), sp), device_id_type=MESH,
         ).start()
+
+    def send_half(half):
         relaxed = levels[4, half_rows(half)].reshape(64, Z)
         carried = product(relaxed, high[0], low[0]).reshape(8, Y, Z)
         term = levels[8, half_rows(half)] - jnp.where(head, 0.0, carried)
@@ -209,8 +288,8 @@
             scan.at[half, 0, pl.ds(pl.multiple_of((place + PAD) * 8, 8), 8)],
             own_sem.at[half, 0],
         ).start()
-        for i in range(1, NT):
-            peer = (tm + i) & (NT - 1)
+        for move in PEERS:
+            peer = moved(tm, *move)
             pltpu.make_async_remote_copy(
                 src_ref=outbox.at[half, pl.ds(pl.multiple_of(peer * 8, 8), 8)],
                 dst_ref=scan.at[half, 0, pl.ds(pl.multiple_of((place + PAD) * 8, 8), 8)],
@@ -227,40 +306,53 @@
     keep_factor(H, X)
     for level in range(1, 8):
         step(level, H + level, X - 2 * level)
-    hear(0)
-    tell(1)
+    send_relaxed(0)
+    pass_on(1)
+    pass_on(0)
+
+    @pl.when(middle)
+    def _():
+        pl.semaphore_wait(known.at[1], NS - 1)
+        tell(2, [tm], [slab for slab in range(NS) if slab != MIDDLE])
+
     wait_halo(1)
     keep_factor(H + X, 7)
     for level in range(1, 9):
         step(level, H + X - level, 8)
+    send_relaxed(1)
     send_half(UPPER)
-    hear(1)
-    tell(2)
     wait_halo(0)
     keep_factor(1, 7)
     for level in range(1, 9):
         step(level, level, 8)
+    send_relaxed(2)
     send_half(LOWER)
-    hear(2)
-    tell(3)
 
     total = jnp.zeros((Y, Z), F32)
-    for half in (UPPER, LOWER):
-        pltpu.make_async_copy(beside.at[half], beside.at[half], beside_recv.at[half]).wait()
+    for piece, (first, count) in enumerate(pieces):
+        rows = beside.at[pl.ds(first, count)]
+        pltpu.make_async_copy(rows, rows, beside_recv.at[piece]).wait()
 
         def add(i, sums):
-            residual = levels[8, H + half * 8 + i] - beside[half, i]
+            residual = levels[8, H + i] - beside[i]
             return sums + residual * residual
 
-        total = lax.fori_loop(0, 8, add, total)
+        total = lax.fori_loop(first, first + count, add, total, unroll=True)
     lanes = total[:, 0:128] + total[:, 128:256] + total[:, 256:384] + total[:, 384:512]
     partial[...] = jnp.sum(lanes, axis=0, keepdims=True)
-    hear(3)
+    @pl.when(jnp.logical_not(middle))
+    def _():
+        pl.semaphore_wait(known.at[2], 1)
+
     for i in range(NS):
         pltpu.make_async_remote_copy(
             src_ref=partial, dst_ref=gathered.at[sp], send_sem=norm_send, recv_sem=norm_recv,
             device_id=((tm + 2) & (NT - 1), (sp + i) & (NS - 1)), device_id_type=MESH,
         ).start()
+
+    @pl.when(jnp.logical_not(early))
+    def _():
+        powers()
 
     def view(half, stage, first, slices):
         pieces = [
@@ -293,8 +385,8 @@
         pltpu.make_async_copy(
             result.at[half, pl.ds(pl.multiple_of(tm * 8, 8), 8)], here, own_sem.at[half, 1]
         ).start()
-        for i in range(1, NT):
-            peer = (tm + i) & (NT - 1)
+        for move in PEERS:
+            peer = moved(tm, *move)
             pltpu.make_async_remote_copy(
                 src_ref=result.at[half, pl.ds(pl.multiple_of(peer * 8, 8), 8)], dst_ref=here,
                 send_sem=back_send.at[half], recv_sem=back_recv.at[half],
@@ -313,10 +405,12 @@
         pltpu.make_async_copy(others, others, back_recv.at[half]).wait()
         pltpu.make_async_copy(others, others, turn_send.at[half]).wait()
         pltpu.make_async_copy(others, others, back_send.at[half]).wait()
-        pltpu.make_async_copy(beside.at[half], beside.at[half], beside_send.at[half]).wait()
     pltpu.make_async_copy(gathered, gathered, norm_send).wait()
+    for piece, (first, count) in enumerate(pieces):
+        rows = beside.at[pl.ds(first, count)]
+        pltpu.make_async_copy(rows, rows, beside_send.at[piece]).wait()
     for side in sides:
-        for index, (buffer, count) in enumerate(((levels.at[0], 8), (force, 7), (walls, 7))):
+        for index, (buffer, count) in enumerate(((levels.at[0], 8), (force, 7), (force, 7))):
             there = pl.ds(0, count)
             pltpu.make_async_copy(buffer.at[there], buffer.at[there], halo_send.at[side, index]).wait()
 
@@ -350,11 +444,11 @@
             pltpu.VMEM((2, NT * 8, 128), F32),
             pltpu.VMEM((2, 3, (PAD + NT) * 8, 128), F32),
             pltpu.VMEM((2, NT * 8, 128), F32),
-            pltpu.VMEM((2, 8, Y, Z), F32),
+            pltpu.VMEM((X, Y, Z), F32),
             pltpu.VMEM((1, 128), F32),
             pltpu.VMEM((NS, 1, 128), F32),
             dma((6,)), dma((2, 4)), dma((2, 4)), dma((2,)), dma((2,)), dma((2,)), dma((2,)),
-            dma((2, 2)), dma((2,)), dma((2,)), dma, dma, pltpu.SemaphoreType.REGULAR((4,)),
+            dma((2, 2)), dma((3,)), dma((3,)), dma, dma, pltpu.SemaphoreType.REGULAR((3,)),
         ],
         compiler_params=pltpu.CompilerParams(
             collective_id=0, has_side_effects=True, vmem_limit_bytes=63 * 1024 * 1024

time: 48.4 us -> 42.4 us (0.88)
  Pallas kernels: 44.7 us -> 38.7 us
    pallas_call x1, Pallas kernels: 44.7 us -> 38.7 us  [shards(): pl.pallas_call(kernel, out_shape=(jax.ShapeDtypeStruct((X * Y * Z // 128,...]
where the time goes in v3:
time: 42.4 us; the launch traced here: 42.2 us
  Pallas kernels  38.7 us (91%)
  local copies, waits for them, and re-layouts  2.89 us (7%)
  between operations  0.64 us (2%)
    pallas_call x1, Pallas kernels, shards(): pl.pallas_call(kernel, out_shape=(jax.ShapeDtypeStruct((X * Y * Z // 128,...  38.7 us
    reshape x1, local copies, waits for them, and re-layouts, shards(): return (landed.reshape(1, X, Y, Z), norm[0, 0:1])  1.69 us
    slice x1, local copies, waits for them, and re-layouts, shards(): return (landed.reshape(1, X, Y, Z), norm[0, 0:1])  1.2 us

profile of v3, /device:TPU:1, one launch (start us, length us, event | category | flops | bytes accessed | tf_op | source)
XLA Modules:
  0.0 42.2 jit_solution(7868776436055895469)
XLA Ops:
  0.6 38.7 %shard_map.86 = (f32[512,128]{1,0:T(8,128)}, f32[8,128]{1,0:T(8,128)}) custom-call(f32[16,8,512]{2,1,0:T(8,128)} %initial.1, f32[16,8,512]{2,1,0:T(8,128)} %stale.1, f32[1,16,8,512]{3,2,1,0:T(8,128)} %guess.1, f32[16,8,512]{2,1,0:T(8,128)} %forcing.1, s32[16,8,512]{2,1,0:T(8,128)} %classes.1, f32[4]{0:T(128)} %damping_table.1, f32[512,512]{1,0:T(8,128)} %coarse.1), custom_call_target="tpu_custom_call" | custom-call | tf_op jit(solution)/shard_map/pallas_call | solution.py:427
  39.3 1.2 %slice.3 = f32[1,1]{1,0:T(1,128)} slice(f32[8,128]{1,0:T(8,128)} %get-tuple-element.5), slice={[0:1], [0:1]} | slice | bytes 8 | tf_op jit(solution)/shard_map/slice | solution.py:457
  40.5 1.7 %reshape.7 = f32[1,16,8,512]{3,2,1,0:T(8,128)} reshape(f32[512,128]{1,0:T(8,128)} %get-tuple-element.4) | data formatting | bytes 524288 | tf_op jit(solution)/shard_map/reshape | solution.py:457

commit v4 on v3

--- a/solution.py
+++ b/solution.py
@@ -12,7 +12,7 @@
 F32, BF16 = jnp.float32, jnp.bfloat16
 NT, NS = 32, 16
 X, Y, Z = 16, 8, 512
-MIDDLE = 4
+HEAD, MIDDLE = 1, 4
 H = 8
 PAD = 4
 BLOCK = 256
@@ -41,8 +41,7 @@
     [(dy, dx, dc) for dy in range(4) for dx in range(4) for dc in range(2)][1:],
     key=lambda d: -min(d[0], 4 - d[0]) - min(d[1], 4 - d[1]),
 )
-LINE = [(0, dx, dc) for dx in range(4) for dc in range(2)][1:]
-BESIDE = LINE + [(dy, 0, dc) for dy in range(1, 4) for dc in range(2)]
+OTHER = (0, 0, 1)
 
 
 def kernel(
@@ -63,15 +62,29 @@
 
     greet(tm, up)
     greet(tm, down)
-    for move in BESIDE:
-        greet(moved(tm, *move), sp)
-    middle = sp == MIDDLE
-
-    @pl.when(middle)
-    def _():
-        for i in range(2, NS - 1):
-            greet(tm, MIDDLE + i & (NS - 1))
-
+    greet(tm ^ 1, sp)
+    head_of_plane, middle = tm == HEAD, sp == MIDDLE
+
+    @pl.when(head_of_plane)
+    def _():
+        for move in PEERS:
+            if move != OTHER:
+                greet(moved(tm, *move), sp)
+
+        @pl.when(middle)
+        def _():
+            for i in range(2, NS - 1):
+                greet(tm, MIDDLE + i & (NS - 1))
+
+    first_in_line, last_in_line = (tm & 7) == 0, (tm & 7) == 7
+
+    @pl.when(((tm & 1) == 1) & jnp.logical_not(last_in_line))
+    def _():
+        greet((tm + 1) & (NT - 1), sp)
+
+    @pl.when(first_in_line)
+    def _():
+        greet((tm + NT - 1) & (NT - 1), sp)
 
     own = pl.ds(H, X)
     loads = [
@@ -135,8 +148,10 @@
         split_prop()
         powers()
 
-    beside_middle = (sp >= MIDDLE - 1) & (sp <= MIDDLE + 1)
-    pl.semaphore_wait(barrier, 2 + len(BESIDE) + jnp.where(beside_middle, 0, 1))
+    from_head = jnp.where((tm == HEAD) | (tm == HEAD ^ 1), 0, 1)
+    from_middle = jnp.where(head_of_plane & ((sp < MIDDLE - 1) | (sp > MIDDLE + 1)), 1, 0)
+    from_line = jnp.where((((tm & 1) == 0) & jnp.logical_not(first_in_line)) | last_in_line, 1, 0)
+    pl.semaphore_wait(barrier, 3 + from_head + from_middle + from_line)
 
     def tell(index, slices, slabs):
         for peer in slices:
@@ -178,17 +193,19 @@
         def _():
             halo(initial, levels.at[9], side, 3, 4).start()
 
-    tell(0, [moved(tm, *move) for move in LINE], [sp])
+    @pl.when(jnp.logical_not(head_of_plane))
+    def _():
+        tell(0, [HEAD], [sp])
+
+    @pl.when(last_in_line)
+    def _():
+        tell(5, [(tm + 1) & (NT - 1)], [sp])
+
+    plane = [moved(tm, *move) for move in PEERS]
 
     @pl.when(jnp.logical_not(early))
     def _():
         load()
-
-    pl.semaphore_wait(known.at[0], len(LINE))
-
-    @pl.when(jnp.logical_not(middle))
-    def _():
-        tell(1, [tm], [MIDDLE])
 
     @pl.when(jnp.logical_not(early))
     def _():
@@ -306,20 +323,33 @@
     keep_factor(H, X)
     for level in range(1, 8):
         step(level, H + level, X - 2 * level)
+    @pl.when(first_in_line)
+    def _():
+        pl.semaphore_wait(known.at[5], 1)
+
     send_relaxed(0)
     pass_on(1)
     pass_on(0)
 
-    @pl.when(middle)
-    def _():
-        pl.semaphore_wait(known.at[1], NS - 1)
-        tell(2, [tm], [slab for slab in range(NS) if slab != MIDDLE])
+    @pl.when(head_of_plane)
+    def _():
+        pl.semaphore_wait(known.at[0], NT - 1)
+        tell(1, plane, [sp])
+
+        @pl.when(jnp.logical_not(middle))
+        def _():
+            tell(2, [HEAD], [MIDDLE])
 
     wait_halo(1)
     keep_factor(H + X, 7)
     for level in range(1, 9):
         step(level, H + X - level, 8)
     send_relaxed(1)
+
+    @pl.when(jnp.logical_not(head_of_plane))
+    def _():
+        pl.semaphore_wait(known.at[1], 1)
+
     send_half(UPPER)
     wait_halo(0)
     keep_factor(1, 7)
@@ -328,6 +358,19 @@
     send_relaxed(2)
     send_half(LOWER)
 
+    @pl.when(head_of_plane)
+    def _():
+        @pl.when(middle)
+        def _():
+            pl.semaphore_wait(known.at[2], NS - 1)
+            tell(3, [HEAD], [slab for slab in range(NS) if slab != MIDDLE])
+
+        @pl.when(jnp.logical_not(middle))
+        def _():
+            pl.semaphore_wait(known.at[3], 1)
+
+        tell(4, plane, [sp])
+
     total = jnp.zeros((Y, Z), F32)
     for piece, (first, count) in enumerate(pieces):
         rows = beside.at[pl.ds(first, count)]
@@ -340,9 +383,9 @@
         total = lax.fori_loop(first, first + count, add, total, unroll=True)
     lanes = total[:, 0:128] + total[:, 128:256] + total[:, 256:384] + total[:, 384:512]
     partial[...] = jnp.sum(lanes, axis=0, keepdims=True)
-    @pl.when(jnp.logical_not(middle))
-    def _():
-        pl.semaphore_wait(known.at[2], 1)
+    @pl.when(jnp.logical_not(head_of_plane))
+    def _():
+        pl.semaphore_wait(known.at[4], 1)
 
     for i in range(NS):
         pltpu.make_async_remote_copy(
@@ -448,10 +491,10 @@
             pltpu.VMEM((1, 128), F32),
             pltpu.VMEM((NS, 1, 128), F32),
             dma((6,)), dma((2, 4)), dma((2, 4)), dma((2,)), dma((2,)), dma((2,)), dma((2,)),
-            dma((2, 2)), dma((3,)), dma((3,)), dma, dma, pltpu.SemaphoreType.REGULAR((3,)),
+            dma((2, 2)), dma((3,)), dma((3,)), dma, dma, pltpu.SemaphoreType.REGULAR((6,)),
         ],
         compiler_params=pltpu.CompilerParams(
-            collective_id=0, has_side_effects=True, vmem_limit_bytes=63 * 1024 * 1024
+            collective_id=0, has_side_effects=True, vmem_limit_bytes=54900 * 1024
         ),
     )(initial, stale_start, guess, forcing, wall_class, damping_table, coarse_prop)
     return landed.reshape(1, X, Y, Z), norm[0, 0:1]

time: 42.4 us -> 40 us (0.943)
  Pallas kernels: 38.7 us -> 37.3 us
  local copies, waits for them, and re-layouts: 2.89 us -> 1.9 us
    pallas_call x1, Pallas kernels: 38.7 us -> 37.3 us  [shards(): pl.pallas_call(kernel, out_shape=(jax.ShapeDtypeStruct((X * Y * Z // 128,...]
    reshape x1, local copies, waits for them, and re-layouts: 1.69 us -> 0.74 us  [shards(): return (landed.reshape(1, X, Y, Z), norm[0, 0:1])]
    slice x1, local copies, waits for them, and re-layouts: 1.2 us -> 0.51 us  [shards(): return (landed.reshape(1, X, Y, Z), norm[0, 0:1])]
    unnamed x0 -> x2, local copies, waits for them, and re-layouts: none -> 0.65 us
where the time goes in v4:
time: 40 us; the launch traced here: 39.9 us
  Pallas kernels  37.3 us (93%)
  local copies, waits for them, and re-layouts  1.9 us (5%)
  between operations  0.65 us (2%)
    pallas_call x1, Pallas kernels, shards(): pl.pallas_call(kernel, out_shape=(jax.ShapeDtypeStruct((X * Y * Z // 128,...  37.3 us

profile of v4, /device:TPU:1, one launch (start us, length us, event | category | flops | bytes accessed | tf_op | source)
XLA Modules:
  0.0 39.9 jit_solution(16673536139675481065)
XLA Ops:
  0.6 0.0 copy-start
  0.6 0.6 %copy-done = f32[4]{0:T(128)S(1)} copy-done((f32[4]{0:T(128)S(1)}, f32[4]{0:T(128)}, u32[]{:S(2)}) %copy-start) | copy-done | bytes 40
  1.3 37.3 %shard_map.86 = (f32[512,128]{1,0:T(8,128)S(1)}, f32[8,128]{1,0:T(8,128)S(1)}) custom-call(f32[16,8,512]{2,1,0:T(8,128)} %initial.1, f32[16,8,512]{2,1,0:T(8,128)} %stale.1, f32[1,16,8,512]{3,2,1,0:T(8,128)} %guess.1, f32[16,8,512]{2,1,0:T(8,128)} %forcing.1, s32[16,8,512]{2,1,0:T(8,128)} %classes.1, f32[4]{0:T(128)S(1)} %copy-done, f32[512,512]{1,0:T(8,128)} %coarse.1), custom_call_target="tpu_custom_call" | custom-call | tf_op jit(solution)/shard_map/pallas_call | solution.py:470
  38.6 0.5 %slice.3 = f32[1,1]{1,0:T(1,128)} slice(f32[8,128]{1,0:T(8,128)S(1)} %get-tuple-element.5), slice={[0:1], [0:1]} | slice | bytes 8 | tf_op jit(solution)/shard_map/slice | solution.py:500
  39.1 0.7 %reshape.7 = f32[1,16,8,512]{3,2,1,0:T(8,128)} reshape(f32[512,128]{1,0:T(8,128)S(1)} %get-tuple-element.4) | data formatting | bytes 524288 | tf_op jit(solution)/shard_map/reshape | solution.py:500
Async XLA Ops:
  0.6 0.7 %copy-start = (f32[4]{0:T(128)S(1)}, f32[4]{0:T(128)}, u32[]{:S(2)}) copy-start(f32[4]{0:T(128)} %damping_table.1) | copy-start | bytes 52

commit v5 on v4

--- a/solution.py
+++ b/solution.py
@@ -12,6 +12,7 @@
 F32, BF16 = jnp.float32, jnp.bfloat16
 NT, NS = 32, 16
 X, Y, Z = 16, 8, 512
+FIRST = 4
 HEAD, MIDDLE = 1, 4
 H = 8
 PAD = 4
@@ -76,6 +77,13 @@
             for i in range(2, NS - 1):
                 greet(tm, MIDDLE + i & (NS - 1))
 
+    first_slabs, early = sp < FIRST, sp < NS // 2
+
+    @pl.when(first_slabs)
+    def _():
+        for slab in range(FIRST, NS):
+            greet((tm + NT - 2) & (NT - 1), slab)
+
     first_in_line, last_in_line = (tm & 7) == 0, (tm & 7) == 7
 
     @pl.when(((tm & 1) == 1) & jnp.logical_not(last_in_line))
@@ -100,7 +108,9 @@
         copy_table.start()
         for copy in loads:
             copy.start()
-        pltpu.make_async_copy(initial, levels.at[9, own], local_sem.at[4]).start()
+        @pl.when(head)
+        def _():
+            pltpu.make_async_copy(initial, levels.at[9, own], local_sem.at[4]).start()
 
         @pl.when(last)
         def _():
@@ -125,8 +135,8 @@
 
         lax.fori_loop(0, Z // 128, one, 0)
 
-    def powers():
-        for power in range(1, 4):
+    def powers(first, end):
+        for power in range(first, end):
             def square(i, carry):
                 rows = pl.ds(pl.multiple_of(i * BLOCK, BLOCK), BLOCK)
                 first, second = high[power - 1, rows, :], low[power - 1, rows, :]
@@ -140,18 +150,16 @@
 
             lax.fori_loop(0, Z // BLOCK, square, 0)
 
-    early = sp < NS // 2
-
     @pl.when(early)
     def _():
         load()
         split_prop()
-        powers()
+        powers(1, 4)
 
     from_head = jnp.where((tm == HEAD) | (tm == HEAD ^ 1), 0, 1)
     from_middle = jnp.where(head_of_plane & ((sp < MIDDLE - 1) | (sp > MIDDLE + 1)), 1, 0)
     from_line = jnp.where((((tm & 1) == 0) & jnp.logical_not(first_in_line)) | last_in_line, 1, 0)
-    pl.semaphore_wait(barrier, 3 + from_head + from_middle + from_line)
+    pl.semaphore_wait(barrier, 3 + from_head + from_middle + from_line + jnp.where(first_slabs, 0, FIRST))
 
     def tell(index, slices, slabs):
         for peer in slices:
@@ -210,6 +218,7 @@
     @pl.when(jnp.logical_not(early))
     def _():
         split_prop()
+        powers(1, 3)
 
     lane = lax.broadcasted_iota(jnp.int32, (1, Y, Z), 2)
     row = lax.broadcasted_iota(jnp.int32, (1, Y, Z), 1)
@@ -225,7 +234,7 @@
             keep[start + i] = (1.0 - 6.0 * COUPLING) - damping
             return carry
 
-        lax.fori_loop(0, count, one, 0)
+        lax.fori_loop(0, count, one, 0, unroll=True)
 
     second_source = jnp.where(head, 9, 4)
 
@@ -269,10 +278,14 @@
         def _():
             onward(walls).start()
 
-    def wait_halo(side):
-        for index, (buffer, count) in ((0, (levels.at[0], 8)), (2, (force, 7))):
-            there = end(side, count)
-            pltpu.make_async_copy(buffer.at[there], buffer.at[there], halo_recv.at[side, index]).wait()
+    def wait_statics(side):
+        there = end(side, 7)
+        pltpu.make_async_copy(force.at[there], force.at[there], halo_recv.at[side, 2]).wait()
+        keep_factor(H + X if side == 1 else 1, 7)
+
+    def wait_field(side):
+        there = end(side, 8)
+        pltpu.make_async_copy(levels.at[0, there], levels.at[0, there], halo_recv.at[side, 0]).wait()
 
         @pl.when(head)
         def _():
@@ -316,7 +329,11 @@
 
     for copy in (copy_table, field, *loads[:2]):
         copy.wait()
-    pltpu.make_async_copy(initial, levels.at[9, own], local_sem.at[4]).wait()
+
+    @pl.when(head)
+    def _():
+        pltpu.make_async_copy(initial, levels.at[9, own], local_sem.at[4]).wait()
+
     for half in range(2):
         for stage in range(3):
             scan[half, stage, 0 : PAD * 8, :] = jnp.zeros((PAD * 8, 128), F32)
@@ -340,62 +357,103 @@
         def _():
             tell(2, [HEAD], [MIDDLE])
 
-    wait_halo(1)
-    keep_factor(H + X, 7)
-    for level in range(1, 9):
-        step(level, H + X - level, 8)
-    send_relaxed(1)
-
-    @pl.when(jnp.logical_not(head_of_plane))
-    def _():
-        pl.semaphore_wait(known.at[1], 1)
-
-    send_half(UPPER)
-    wait_halo(0)
-    keep_factor(1, 7)
-    for level in range(1, 9):
-        step(level, level, 8)
-    send_relaxed(2)
-    send_half(LOWER)
-
-    @pl.when(head_of_plane)
-    def _():
-        @pl.when(middle)
+    def steps(side, first, last):
+        for level in range(first, last + 1):
+            step(level, H + X - level if side == 1 else level, 8)
+
+    def first_sweep(side):
+        wait_field(side)
+        steps(side, 1, 4)
+        send_relaxed(1 if side == 1 else 2)
+
+    def hear_plane():
+        @pl.when(jnp.logical_not(head_of_plane))
+        def _():
+            pl.semaphore_wait(known.at[1], 1)
+
+    def pass_world():
+        @pl.when(head_of_plane)
+        def _():
+            @pl.when(jnp.logical_not(middle))
+            def _():
+                pl.semaphore_wait(known.at[3], 1)
+
+            tell(4, plane, [sp])
+
+    @pl.when(early)
+    def _():
+        wait_statics(1)
+        first_sweep(1)
+        steps(1, 5, 8)
+        hear_plane()
+        send_half(UPPER)
+
+        @pl.when(head_of_plane & middle)
         def _():
             pl.semaphore_wait(known.at[2], NS - 1)
             tell(3, [HEAD], [slab for slab in range(NS) if slab != MIDDLE])
 
-        @pl.when(jnp.logical_not(middle))
-        def _():
-            pl.semaphore_wait(known.at[3], 1)
-
-        tell(4, plane, [sp])
-
-    total = jnp.zeros((Y, Z), F32)
-    for piece, (first, count) in enumerate(pieces):
-        rows = beside.at[pl.ds(first, count)]
-        pltpu.make_async_copy(rows, rows, beside_recv.at[piece]).wait()
-
-        def add(i, sums):
-            residual = levels[8, H + i] - beside[i]
-            return sums + residual * residual
-
-        total = lax.fori_loop(first, first + count, add, total, unroll=True)
-    lanes = total[:, 0:128] + total[:, 128:256] + total[:, 256:384] + total[:, 384:512]
-    partial[...] = jnp.sum(lanes, axis=0, keepdims=True)
-    @pl.when(jnp.logical_not(head_of_plane))
-    def _():
-        pl.semaphore_wait(known.at[4], 1)
-
-    for i in range(NS):
-        pltpu.make_async_remote_copy(
-            src_ref=partial, dst_ref=gathered.at[sp], send_sem=norm_send, recv_sem=norm_recv,
-            device_id=((tm + 2) & (NT - 1), (sp + i) & (NS - 1)), device_id_type=MESH,
-        ).start()
+        wait_statics(0)
+        first_sweep(0)
+        steps(0, 5, 8)
+        send_half(LOWER)
 
     @pl.when(jnp.logical_not(early))
     def _():
-        powers()
+        wait_statics(1)
+        wait_statics(0)
+        first_sweep(1)
+        first_sweep(0)
+        steps(1, 5, 8)
+        hear_plane()
+        send_half(UPPER)
+        pass_world()
+        steps(0, 5, 8)
+        send_half(LOWER)
+
+    def sum_squares():
+        total = jnp.zeros((Y, Z), F32)
+        for piece, (first, count) in enumerate(pieces):
+            rows = beside.at[pl.ds(first, count)]
+            pltpu.make_async_copy(rows, rows, beside_recv.at[piece]).wait()
+
+            def add(i, sums):
+                residual = levels[8, H + i] - beside[i]
+                return sums + residual * residual
+
+            total = lax.fori_loop(first, first + count, add, total, unroll=True)
+        lanes = total[:, 0:128] + total[:, 128:256] + total[:, 256:384] + total[:, 384:512]
+        partial[...] = jnp.sum(lanes, axis=0, keepdims=True)
+
+    def send_squares(slabs):
+        for slab in slabs:
+            pltpu.make_async_remote_copy(
+                src_ref=partial, dst_ref=gathered.at[sp], send_sem=norm_send, recv_sem=norm_recv,
+                device_id=((tm + 2) & (NT - 1), slab), device_id_type=MESH,
+            ).start()
+
+    def hear_all():
+        @pl.when(jnp.logical_not(head_of_plane))
+        def _():
+            pl.semaphore_wait(known.at[4], 1)
+
+    @pl.when(jnp.logical_not(first_slabs))
+    def _():
+        sum_squares()
+        send_squares(range(FIRST))
+
+    @pl.when(early)
+    def _():
+        pass_world()
+
+    @pl.when(jnp.logical_not(early))
+    def _():
+        powers(3, 4)
+
+    @pl.when(jnp.logical_not(first_slabs))
+    def _():
+        hear_all()
+        send_squares(range(FIRST, NS))
 
     def view(half, stage, first, slices):
         pieces = [
@@ -435,6 +493,12 @@
                 send_sem=back_send.at[half], recv_sem=back_recv.at[half],
                 device_id=(peer, sp), device_id_type=MESH,
             ).start()
+
+    @pl.when(first_slabs)
+    def _():
+        sum_squares()
+        hear_all()
+        send_squares(range(NS))
 
     pltpu.make_async_copy(gathered, gathered, norm_recv).wait()
     squares = jnp.sum(gathered[...], axis=0)

time: 40 us -> 39.4 us (0.985)
  Pallas kernels: 37.3 us -> 36.6 us
    pallas_call x1, Pallas kernels: 37.3 us -> 36.6 us  [shards(): pl.pallas_call(kernel, out_shape=(jax.ShapeDtypeStruct((X * Y * Z // 128,...]
where the time goes in v5:
time: 39.4 us; the launch traced here: 39.2 us
  Pallas kernels  36.6 us (93%)
  local copies, waits for them, and re-layouts  1.9 us (5%)
  between operations  0.65 us (2%)
    pallas_call x1, Pallas kernels, shards(): pl.pallas_call(kernel, out_shape=(jax.ShapeDtypeStruct((X * Y * Z // 128,...  36.6 us

profile of v5, /device:TPU:1, one launch (start us, length us, event | category | flops | bytes accessed | tf_op | source)
XLA Modules:
  0.0 39.2 jit_solution(16134173661083832889)
XLA Ops:
  0.6 0.0 copy-start
  0.6 0.6 %copy-done = f32[4]{0:T(128)S(1)} copy-done((f32[4]{0:T(128)S(1)}, f32[4]{0:T(128)}, u32[]{:S(2)}) %copy-start) | copy-done | bytes 40
  1.3 36.6 %shard_map.86 = (f32[512,128]{1,0:T(8,128)S(1)}, f32[8,128]{1,0:T(8,128)S(1)}) custom-call(f32[16,8,512]{2,1,0:T(8,128)} %initial.1, f32[16,8,512]{2,1,0:T(8,128)} %stale.1, f32[1,16,8,512]{3,2,1,0:T(8,128)} %guess.1, f32[16,8,512]{2,1,0:T(8,128)} %forcing.1, s32[16,8,512]{2,1,0:T(8,128)} %classes.1, f32[4]{0:T(128)S(1)} %copy-done, f32[512,512]{1,0:T(8,128)} %coarse.1), custom_call_target="tpu_custom_call" | custom-call | tf_op jit(solution)/shard_map/pallas_call | solution.py:534
  37.9 0.5 %slice.3 = f32[1,1]{1,0:T(1,128)} slice(f32[8,128]{1,0:T(8,128)S(1)} %get-tuple-element.5), slice={[0:1], [0:1]} | slice | bytes 8 | tf_op jit(solution)/shard_map/slice | solution.py:564
  38.5 0.7 %reshape.7 = f32[1,16,8,512]{3,2,1,0:T(8,128)} reshape(f32[512,128]{1,0:T(8,128)S(1)} %get-tuple-element.4) | data formatting | bytes 524288 | tf_op jit(solution)/shard_map/reshape | solution.py:564
Async XLA Ops:
  0.6 0.7 %copy-start = (f32[4]{0:T(128)S(1)}, f32[4]{0:T(128)}, u32[]{:S(2)}) copy-start(f32[4]{0:T(128)} %damping_table.1) | copy-start | bytes 52

commit v6 on v5

--- a/solution.py
+++ b/solution.py
@@ -380,37 +380,6 @@
 
             tell(4, plane, [sp])
 
-    @pl.when(early)
-    def _():
-        wait_statics(1)
-        first_sweep(1)
-        steps(1, 5, 8)
-        hear_plane()
-        send_half(UPPER)
-
-        @pl.when(head_of_plane & middle)
-        def _():
-            pl.semaphore_wait(known.at[2], NS - 1)
-            tell(3, [HEAD], [slab for slab in range(NS) if slab != MIDDLE])
-
-        wait_statics(0)
-        first_sweep(0)
-        steps(0, 5, 8)
-        send_half(LOWER)
-
-    @pl.when(jnp.logical_not(early))
-    def _():
-        wait_statics(1)
-        wait_statics(0)
-        first_sweep(1)
-        first_sweep(0)
-        steps(1, 5, 8)
-        hear_plane()
-        send_half(UPPER)
-        pass_world()
-        steps(0, 5, 8)
-        send_half(LOWER)
-
     def sum_squares():
         total = jnp.zeros((Y, Z), F32)
         for piece, (first, count) in enumerate(pieces):
@@ -432,12 +401,45 @@
                 device_id=((tm + 2) & (NT - 1), slab), device_id_type=MESH,
             ).start()
 
+    @pl.when(early)
+    def _():
+        wait_statics(1)
+        first_sweep(1)
+        steps(1, 5, 8)
+        hear_plane()
+        send_half(UPPER)
+
+        @pl.when(head_of_plane & middle)
+        def _():
+            pl.semaphore_wait(known.at[2], NS - 1)
+            tell(3, [HEAD], [slab for slab in range(NS) if slab != MIDDLE])
+
+        wait_statics(0)
+        first_sweep(0)
+        steps(0, 5, 8)
+        send_half(LOWER)
+
+    @pl.when(jnp.logical_not(early))
+    def _():
+        wait_statics(1)
+        wait_statics(0)
+        first_sweep(1)
+        first_sweep(0)
+        steps(1, 5, 8)
+        steps(0, 5, 8)
+        sum_squares()
+        send_squares(range(FIRST))
+        hear_plane()
+        send_half(UPPER)
+        pass_world()
+        send_half(LOWER)
+
     def hear_all():
         @pl.when(jnp.logical_not(head_of_plane))
         def _():
             pl.semaphore_wait(known.at[4], 1)
 
-    @pl.when(jnp.logical_not(first_slabs))
+    @pl.when(early & jnp.logical_not(first_slabs))
     def _():
         sum_squares()
         send_squares(range(FIRST))

time: 39.4 us -> 39.4 us (level)
  no operation moved by 1% of the time
where the time goes in v6:
time: 39.4 us; the launch traced here: 39.2 us
  Pallas kernels  36.6 us (93%)
  local copies, waits for them, and re-layouts  1.9 us (5%)
  between operations  0.65 us (2%)
    pallas_call x1, Pallas kernels, shards(): pl.pallas_call(kernel, out_shape=(jax.ShapeDtypeStruct((X * Y * Z // 128,...  36.6 us

profile of v6, /device:TPU:1, one launch (start us, length us, event | category | flops | bytes accessed | tf_op | source)
XLA Modules:
  0.0 39.2 jit_solution(5854561179911627457)
XLA Ops:
  0.6 0.0 copy-start
  0.6 0.6 %copy-done = f32[4]{0:T(128)S(1)} copy-done((f32[4]{0:T(128)S(1)}, f32[4]{0:T(128)}, u32[]{:S(2)}) %copy-start) | copy-done | bytes 40
  1.3 36.6 %shard_map.86 = (f32[512,128]{1,0:T(8,128)S(1)}, f32[8,128]{1,0:T(8,128)S(1)}) custom-call(f32[16,8,512]{2,1,0:T(8,128)} %initial.1, f32[16,8,512]{2,1,0:T(8,128)} %stale.1, f32[1,16,8,512]{3,2,1,0:T(8,128)} %guess.1, f32[16,8,512]{2,1,0:T(8,128)} %forcing.1, s32[16,8,512]{2,1,0:T(8,128)} %classes.1, f32[4]{0:T(128)S(1)} %copy-done, f32[512,512]{1,0:T(8,128)} %coarse.1), custom_call_target="tpu_custom_call" | custom-call | tf_op jit(solution)/shard_map/pallas_call | solution.py:536
  37.9 0.5 %slice.3 = f32[1,1]{1,0:T(1,128)} slice(f32[8,128]{1,0:T(8,128)S(1)} %get-tuple-element.5), slice={[0:1], [0:1]} | slice | bytes 8 | tf_op jit(solution)/shard_map/slice | solution.py:566
  38.5 0.7 %reshape.7 = f32[1,16,8,512]{3,2,1,0:T(8,128)} reshape(f32[512,128]{1,0:T(8,128)S(1)} %get-tuple-element.4) | data formatting | bytes 524288 | tf_op jit(solution)/shard_map/reshape | solution.py:566
Async XLA Ops:
  0.6 0.7 %copy-start = (f32[4]{0:T(128)S(1)}, f32[4]{0:T(128)}, u32[]{:S(2)}) copy-start(f32[4]{0:T(128)} %damping_table.1) | copy-start | bytes 52
